TPU v7x, 32 devices: a whole 2x2x4 slice. The times are simulated.
32 devices in a mesh: expert: 2 (over x), replica: 16 (over z, y, core).
Axes of the slice: x: 2, y: 2, z: 4, core: 2. Of those that a mesh axis runs over, the one named last changes fastest.
Arguments:
- pool: bfloat16 [16, 4096, 2048], P('replica', 'expert'), may hold values from -15 to 15
- row_index: int32 [2, 16, 256], P(None, 'replica'), may hold values from 0 to 4095, as said below
- counts: int32 [2, 16], P('expert', 'replica'), may hold values from 128 to 256, as said below
- targets: bfloat16 [2, 16, 256, 384], P('expert', 'replica'), may hold values from -4 to 4
- weights: float32 [2, 2, 2048, 384], P('expert', None, 'replica'), may hold values from -0.125 to 0.125
- first_moment: float32 [2, 2, 2048, 384], P('expert', None, 'replica'), may hold values from -1.5 to 1.5
- second_moment: float32 [2, 2, 2048, 384], P('expert', None, 'replica'), may hold values from 0.0001 to 0.01
Outputs:
- new_weights: float32 [2, 2, 2048, 384], P('expert', None, 'replica')
- new_first_moment: float32 [2, 2, 2048, 384], P('expert', None, 'replica')
- new_second_moment: float32 [2, 2, 2048, 384], P('expert', None, 'replica')
Inputs may be any that keep to these rules, and one draw needn't show every extreme that they name: `row_index`: for each expert and replica the 256 entries are distinct rows of that replica's 4096 tokens; at most 192 of them lie in any one aligned block of 2048 rows, and some block holds exactly 192 of them. `counts`: at least 128 live slots for each expert on each replica; some expert on some replica has all 256 slots live.
All inputs are finite; a program needn't handle non-finite values.
Results may differ from a plain program's by a relative error of at most 0.0043.
Values may be sent and summed in bfloat16 or wider, within the bound.
No kernel may reach another device: no remote copies, remote signals or barrier semaphores. Data moves between devices by JAX's collectives and lax.ppermute only.
A program may use at most 64 MiB of HBM per device.

v0:
```python
import functools
import math

import jax
import jax.numpy as jnp
from jax import lax
from jax.experimental import pallas as pl
from jax.experimental.pallas import tpu as pltpu
from jax.sharding import PartitionSpec as P

STEP = 3


beta_first = 0.9
beta_second = 0.999
learning_rate = 0.02
decay_rate = 0.1
adam_epsilon = 1e-08
adasum_epsilon = 1e-12

CORE, SIDE = 1, 2
VMEM_LIMIT = 50 * 1024 * 1024
LIGHT = pl.CostEstimate(flops=1, bytes_accessed=1, transcendentals=0)
f32, bf16, i32 = jnp.float32, jnp.bfloat16, jnp.int32


def gathered(x, masks):
    pieces = {0: x}
    for mask in reversed(masks):
        pieces.update({mask | held: swapped(piece, "replica", mask) for held, piece in list(pieces.items())})
    return pieces


def swapped(x, axis, mask):
    return lax.ppermute(x, axis, [(i, i ^ mask) for i in range(lax.axis_size(axis))])


def vmem():
    return pl.BlockSpec(memory_space=pltpu.VMEM)


def smem():
    return pl.BlockSpec(memory_space=pltpu.SMEM)


def params(*arrays):
    total = 0
    for array in arrays:
        *lead, rows, columns = array.shape
        total += math.prod(lead) * -(-rows // 16) * 16 * -(-columns // 128) * 128 * array.dtype.itemsize
    return pltpu.CompilerParams(vmem_limit_bytes=min(2 * total + 4 * 1024 * 1024, VMEM_LIMIT))


def adam_update(gradient, weight, moment_one, moment_two):
    moment_one = beta_first * moment_one + (1.0 - beta_first) * gradient
    moment_two = beta_second * moment_two + (1.0 - beta_second) * gradient * gradient
    first_hat = moment_one / (1.0 - beta_first**STEP)
    second_hat = moment_two / (1.0 - beta_second**STEP)
    weight = weight - learning_rate * (
        first_hat / (jnp.sqrt(second_hat) + adam_epsilon) + decay_rate * weight
    )
    return (weight, moment_one, moment_two)


def grid_iota(shape, dim):
    return lax.broadcasted_iota(i32, shape, dim)


def compacted_rows(listed, block, shard_rows, most):
    slots = listed.shape[1]
    local = listed - block * shard_rows
    held = (local >= 0) & (local < shard_rows)
    down, along = grid_iota((slots, slots), 0), grid_iota((slots, slots), 1)
    held_wide = jnp.broadcast_to(held.astype(i32), (slots, slots))
    held_column = jnp.sum(jnp.where(down == along, held_wide, 0), axis=1, keepdims=True)
    rank = jnp.sum(jnp.where(down < along, jnp.broadcast_to(held_column, (slots, slots)), 0), axis=0, keepdims=True)
    place = jnp.where(held, rank, -1)
    hit = grid_iota((most, slots), 0) == jnp.broadcast_to(place, (most, slots))
    return jnp.sum(jnp.where(hit, jnp.broadcast_to(local + 1, (most, slots)), 0), axis=1, keepdims=True) - 1


def slot_rows(listed, block, shard_rows):
    slots = listed.shape[1]
    local = listed - block * shard_rows
    held = (local >= 0) & (local < shard_rows)
    value = jnp.where(held, local + 1, 0)
    diagonal = grid_iota((slots, slots), 0) == grid_iota((slots, slots), 1)
    return jnp.sum(jnp.where(diagonal, jnp.broadcast_to(value, (slots, slots)), 0), axis=1, keepdims=True) - 1


def slot_ranks(listed, block, shard_rows):
    slots = listed.shape[1]
    local = listed - block * shard_rows
    held = ((local >= 0) & (local < shard_rows)).astype(i32)
    held_wide = jnp.broadcast_to(held, (slots, slots))
    down, along = grid_iota((slots, slots), 0), grid_iota((slots, slots), 1)
    rank = jnp.sum(jnp.where(along < down, held_wide, 0), axis=1, keepdims=True)
    own = jnp.sum(jnp.where(along == down, held_wide, 0), axis=1, keepdims=True)
    return jnp.where(own > 0, rank, -1)


def one_hot(column, width):
    return (grid_iota((column.shape[0], width), 1) == column).astype(f32).astype(bf16)


def pick_kernel(experts, most, shard_rows, where_ref, index_ref, pick_ref):
    slots = index_ref.shape[1]
    me = where_ref[0]
    pick_ref[:slots] = one_hot(slot_rows(index_ref[pl.ds(me, 1), :], me, shard_rows), shard_rows)
    for mask in range(1, experts):
        listed = index_ref[pl.ds(me ^ mask, 1), :]
        first = slots + (mask - 1) * most
        pick_ref[first : first + most] = one_hot(compacted_rows(listed, me, shard_rows, most), shard_rows)


def picks_of(where, index, experts, most, shard_rows):
    return pl.pallas_call(
        functools.partial(pick_kernel, experts, most, shard_rows),
        out_shape=jax.ShapeDtypeStruct((index.shape[1] + (experts - 1) * most, shard_rows), bf16),
        in_specs=[smem(), vmem()],
        out_specs=vmem(),
        compiler_params=params(jax.ShapeDtypeStruct((2 * most, shard_rows), f32)),
        cost_estimate=LIGHT,
        name="row_picks",
    )(where, index)


def listed_kernel(experts, most, where_ref, pick_ref, pool_ref, out_ref, own_ref):
    slots = own_ref.shape[0]
    rows = jnp.dot(pick_ref[...], pool_ref[...], preferred_element_type=f32).astype(bf16)
    own_ref[...] = rows[:slots]
    for mask in range(1, experts):
        out_ref[mask - 1] = rows[slots + (mask - 1) * most : slots + mask * most]


def listed_rows(where, picks, pool, experts, most, part):
    shard_rows, width = pool.shape
    slots = picks.shape[0] - (experts - 1) * most
    steps = 2
    chunk = width // (2 * steps)
    return pl.pallas_call(
        functools.partial(listed_kernel, experts, most),
        out_shape=[
            jax.ShapeDtypeStruct((experts - 1, most, width // 2), bf16),
            jax.ShapeDtypeStruct((slots, width // 2), bf16),
        ],
        grid_spec=pltpu.PrefetchScalarGridSpec(
            num_scalar_prefetch=1,
            grid=(steps,),
            in_specs=[
                pl.BlockSpec(picks.shape, lambda i, w: (0, 0)),
                pl.BlockSpec((shard_rows, chunk), lambda i, w: (0, (w[1] ^ 1 ^ part) * steps + i)),
            ],
            out_specs=[
                pl.BlockSpec((experts - 1, most, chunk), lambda i, w: (0, 0, i)),
                pl.BlockSpec((slots, chunk), lambda i, w: (0, i)),
            ],
        ),
        compiler_params=pltpu.CompilerParams(vmem_limit_bytes=VMEM_LIMIT),
        cost_estimate=LIGHT,
        name="listed_rows",
    )(where, picks, pool)


def merge_kernel(experts, shard_rows, masks, halves, where_ref, index_ref, own_ref, *refs):
    incoming, sent_refs, block_ref = refs[: experts - 1], refs[experts - 1 : -1], refs[-1]
    me, upper, core = where_ref[0], where_ref[2], where_ref[3]
    most = incoming[0].shape[1]
    block = block_ref.shape[2]
    listed = index_ref[pl.ds(me, 1), :]
    rows = own_ref[...].astype(f32)
    for mask in range(1, experts):
        pick = one_hot(slot_ranks(listed, me ^ mask, shard_rows), most)
        rows = rows + jnp.dot(pick, incoming[mask - 1][0], preferred_element_type=f32)
    rows = rows.astype(bf16)
    for column in range(block_ref.shape[0]):
        block_ref[column] = rows[:, column * block : (column + 1) * block]
    for mask, sent_ref in zip(masks, sent_refs):
        first = ((upper ^ mask) & (halves - 1)) * 4
        for core_mask in range(2):
            for side in range(2):
                sent_ref[core_mask, side] = block_ref[first + 2 * side + (core ^ core_mask)]


def merged_rows(where, index, own, incoming, experts, replicas, shard_rows, masks):
    slots, half = own.shape
    block = 2 * half // replicas
    return pl.pallas_call(
        functools.partial(merge_kernel, experts, shard_rows, masks, replicas // 8),
        out_shape=[jax.ShapeDtypeStruct((2, 2, slots, block), bf16)] * len(masks),
        in_specs=[smem()] + [vmem()] * (experts + 1),
        out_specs=[vmem()] * len(masks),
        scratch_shapes=[pltpu.VMEM((replicas // 2, slots, block), bf16)],
        compiler_params=params(own, own, own, *incoming),
        cost_estimate=LIGHT,
        name="merged_rows",
    )(where, index, own, *incoming)


def forward_kernel(uppers, blocks, where_ref, *refs):
    own, crossed_ref, rest, outs = refs[:uppers], refs[uppers], refs[uppers + 1 :], refs[uppers + 1 + len(blocks.arrays) :]
    side = where_ref[4]
    totals = [jnp.zeros(outs[0].shape, f32) for _ in range(4)]
    for mask in range(uppers):
        peer = crossed_ref.at[mask]
        for side_mask in range(2):
            w = blocks.ref(rest, 4 * mask + 2 * side_mask)
            for rows, first in ((own[mask].at[0], 0), (peer, 2)):
                for matrix in range(2):
                    totals[first + matrix] += jnp.dot(rows[side ^ side_mask], w[matrix], preferred_element_type=f32)
    for out, total in zip(outs, totals):
        out[...] = total


def forward(where, crossed, own, blocks, uppers):
    out = jax.ShapeDtypeStruct((own[0].shape[2], blocks.arrays[0].shape[-1]), f32)
    return pl.pallas_call(
        functools.partial(forward_kernel, uppers, blocks),
        out_shape=[out] * 4,
        in_specs=[smem()] + [vmem()] * (uppers + 1 + len(blocks.arrays)),
        out_specs=[vmem()] * 4,
        compiler_params=params(*own, crossed, *blocks.arrays),
        cost_estimate=LIGHT,
        name="forward_values",
    )(where, *own, crossed, *blocks.arrays)


def delta_kernel(where_ref, count_ref, targets_ref, gate_ref, up_ref, gate_other_ref, up_other_ref, kept_ref, sent_ref):
    side = where_ref[4]
    slots = targets_ref.shape[0]
    gate_value = gate_ref[...] + gate_other_ref[...]
    up_value = up_ref[...] + up_other_ref[...]
    live_count = count_ref[0, 0]
    sigmoid = jax.nn.sigmoid(gate_value)
    activated = gate_value * sigmoid
    silu_slope = sigmoid * (1.0 + gate_value * (1.0 - sigmoid))
    live = (grid_iota((slots, 1), 0) < live_count).astype(f32)
    residual = (activated * up_value - targets_ref[...].astype(f32)) * live / jnp.full((1, 1), live_count, i32).astype(f32)
    gate_delta = (residual * up_value * silu_slope).astype(bf16)
    up_delta = (residual * activated).astype(bf16)
    kept_ref[...] = jnp.where(side == 0, gate_delta, up_delta)
    sent_ref[...] = jnp.where(side == 0, up_delta, gate_delta)


def deltas_of(where, count, targets, values):
    out = jax.ShapeDtypeStruct(targets.shape, bf16)
    return pl.pallas_call(
        delta_kernel,
        out_shape=[out, out],
        in_specs=[smem(), smem()] + [vmem()] * (1 + len(values)),
        out_specs=[vmem()] * 2,
        compiler_params=params(targets, *values),
        cost_estimate=LIGHT,
        name="deltas",
    )(where, count, targets, *values)


def token_contract(left, right):
    return lax.dot_general(left, right, (((0,), (0,)), ((), ())), preferred_element_type=f32)


TILE = 16


class Pieces:
    def __init__(self):
        self.arrays, self.place = [], {}

    def put(self, keys, pieces):
        if isinstance(pieces, list):
            for key, piece in zip(keys, pieces):
                self.place[key] = (len(self.arrays), None)
                self.arrays.append(piece)
            return
        for index, key in enumerate(keys):
            self.place[key] = (len(self.arrays), index)
        self.arrays.append(pieces)

    def ref(self, refs, key):
        array, index = self.place[key]
        return refs[array] if index is None else refs[array].at[index]

    def read(self, refs, key):
        return self.ref(refs, key)[...]


def split_refs(rows, deltas, refs):
    count = len(rows.arrays)
    rest = refs[count:]

    def rows_of(key):
        ref = rows.ref(refs, key)
        return ref.at[0] if len(ref.shape) == 4 else ref

    return rows_of, lambda key: deltas.read(rest, key), rest[len(deltas.arrays) :]


def gram_kernel(replicas, pieces, where_ref, *refs):
    rows, deltas, (gram_ref, table_ref) = split_refs(*pieces, refs)
    me = where_ref[5]
    block = rows(0).shape[2]
    steps = block // TILE
    for mask in range(replicas):
        first = pl.multiple_of((me ^ mask) * TILE, TILE)
        for part in range(2):
            gradient = token_contract(rows(mask)[part], deltas(mask)).astype(bf16)
            for step in range(steps):
                table_ref[part * steps + step, pl.ds(first, TILE), :] = gradient[step * TILE : (step + 1) * TILE]
    size = replicas * TILE
    products = jnp.zeros((size, size), f32)
    for step in range(2 * steps):
        products += lax.dot_general(
            table_ref[step], table_ref[step], (((1,), (1,)), ((), ())), preferred_element_type=f32
        )
    same = (grid_iota((size, size), 0) & (TILE - 1)) == (grid_iota((size, size), 1) & (TILE - 1))
    products = jnp.where(same, products, 0.0)
    down = jnp.concatenate(
        [jnp.sum(products[r * TILE : (r + 1) * TILE], axis=0, keepdims=True) for r in range(replicas)], axis=0
    )
    member = (grid_iota((size, replicas), 0) // TILE == grid_iota((size, replicas), 1)).astype(f32)
    gram_ref[...] = jnp.dot(down, member, preferred_element_type=f32, precision=lax.Precision.HIGHEST)


def gram(where, rows, deltas, replicas):
    depth = 2 * rows.arrays[0].shape[-1]
    hidden = deltas.arrays[0].shape[-1]
    return pl.pallas_call(
        functools.partial(gram_kernel, replicas, (rows, deltas)),
        out_shape=jax.ShapeDtypeStruct((replicas, replicas), f32),
        in_specs=[smem()] + [vmem()] * (len(rows.arrays) + len(deltas.arrays)),
        out_specs=vmem(),
        scratch_shapes=[pltpu.VMEM((depth // TILE, replicas * TILE, hidden), bf16)],
        compiler_params=params(*rows.arrays, *deltas.arrays, jax.ShapeDtypeStruct((replicas * TILE, replicas * TILE), f32)),
        cost_estimate=LIGHT,
        name="gradient_products",
    )(where, *rows.arrays, *deltas.arrays)


def tree_weights(table, replicas):
    down, along = grid_iota((replicas, replicas), 0), grid_iota((replicas, replicas), 1)
    weights = jnp.ones((replicas, 1), f32)
    half = replicas // 2
    while half >= 1:
        same = down == along
        other = ((down + half) & (replicas - 1)) == along
        partner = ((along + half) & (replicas - 1)) == down
        square_down = jnp.sum(jnp.where(same, table, 0.0), axis=1, keepdims=True)
        square_along = jnp.sum(jnp.where(same, table, 0.0), axis=0, keepdims=True)
        inner_down = jnp.sum(jnp.where(other, table, 0.0), axis=1, keepdims=True)
        inner_along = jnp.sum(jnp.where(partner, table, 0.0), axis=0, keepdims=True)
        weight_down = 1.0 - inner_down / (2.0 * square_down + adasum_epsilon)
        weight_along = 1.0 - inner_along / (2.0 * square_along + adasum_epsilon)
        weights = weights * weight_down
        table = weight_down * (table * weight_along)
        table = table + jnp.concatenate([table[half:], table[:half]], axis=0)
        table = table + jnp.concatenate([table[:, half:], table[:, :half]], axis=1)
        half //= 2
    return weights


def combine_kernel(replicas, pieces, where_ref, gram_ref, *refs):
    rows, deltas, (kept_ref, sent_ref, weight_ref) = split_refs(*pieces, refs)
    side, me = where_ref[4], where_ref[5]
    weight_ref[...] = jnp.broadcast_to(tree_weights(gram_ref[...], replicas), weight_ref.shape)
    for ref, part in ((kept_ref, side), (sent_ref, 1 - side)):
        total = jnp.zeros(ref.shape, f32)
        for mask in range(replicas):
            gradient = token_contract(rows(mask)[part], deltas(mask))
            total = total + weight_ref[pl.ds(me ^ mask, 1), 0:1] * gradient
        ref[...] = total


def combine(where, products, rows, deltas):
    replicas = products.shape[0]
    out = jax.ShapeDtypeStruct((rows.arrays[0].shape[-1], deltas.arrays[0].shape[-1]), f32)
    return pl.pallas_call(
        functools.partial(combine_kernel, replicas, (rows, deltas)),
        out_shape=[out, out],
        in_specs=[smem(), vmem()] + [vmem()] * (len(rows.arrays) + len(deltas.arrays)),
        out_specs=[vmem()] * 2,
        scratch_shapes=[pltpu.VMEM((replicas, 128), f32)],
        compiler_params=params(*rows.arrays, *deltas.arrays),
        cost_estimate=LIGHT,
        name="combined_gradient",
    )(where, products, *rows.arrays, *deltas.arrays)


def shards(pool, row_index, counts, targets, weights, first_moment, second_moment):
    replicas = lax.axis_size("replica")
    experts = lax.axis_size("expert")
    uppers = replicas // 4
    position = lax.axis_index("replica")
    expert_position = lax.axis_index("expert")
    core, side, upper = position & 1, position >> 1 & 1, position >> 2
    where = jnp.stack([expert_position, position // (replicas // 2), upper, core, side, position]).astype(i32)
    index = row_index[:, 0, :]
    local_pool = pool[0]
    shard_rows = local_pool.shape[0]
    most = 3 * index.shape[1] // (2 * experts)

    halves = uppers // 2
    upper_masks = [4 << bit for bit in range(uppers.bit_length() - 1)]
    picks = picks_of(where, index, experts, most, shard_rows)
    far, near = list(range(halves, uppers)), list(range(halves))
    packed = [None] * uppers
    for part, masks in enumerate((far, near)):
        outgoing, own = listed_rows(where, picks, local_pool, experts, most, part)
        incoming = [swapped(outgoing[mask - 1 : mask], "expert", mask) for mask in range(1, experts)]
        if part == 0:
            lowered = weights[0].astype(bf16)
            by_upper = gathered(lowered, upper_masks)
            by_upper = [by_upper[4 * mask] for mask in range(uppers)]
            own, picks, *_ = lax.optimization_barrier((own, picks, by_upper[halves], by_upper[1]))
            blocks = Pieces()
            blocks.put([4 * mask for mask in range(uppers)], by_upper)
            besides = []
            for group in (near, far):
                besides.append(swapped(jnp.stack([by_upper[mask] for mask in group]), "replica", SIDE))
                blocks.put([4 * mask | SIDE for mask in group], besides[-1])
        else:
            own, _ = lax.optimization_barrier((own, besides[0]))
        packed[masks[0] : masks[-1] + 1] = merged_rows(
            where, index, own, incoming, experts, replicas, shard_rows, masks
        )

    crossed = swapped(jnp.stack([piece[1] for piece in packed]), "replica", CORE)
    values = forward(where, crossed, packed, blocks, uppers)

    rows = Pieces()
    rows.put([0], [packed[0]])
    others_of = far + near[1:]
    arrived = [swapped(packed[mask], "replica", 4 * mask) for mask in others_of]
    other = swapped(jnp.stack([piece[1] for piece in arrived]), "replica", CORE)
    for mask, piece in zip(others_of, arrived):
        rows.put([4 * mask], [piece])
    rows.put([4 * mask | CORE for mask in others_of], other)
    rows.put([CORE], crossed)
    values = list(values[:2]) + [swapped(value, "replica", CORE) for value in values[2:]]
    kept_delta, sent_delta = deltas_of(where, counts, targets[0, 0], values)
    side_deltas = [kept_delta, swapped(sent_delta, "replica", SIDE)]

    deltas = Pieces()
    far_mask, near_masks = upper_masks[-1], upper_masks[:-1]

    def hold(keys, pieces):
        both = jnp.stack(pieces)
        deltas.put(keys, both)
        across = swapped(both, "replica", CORE)
        deltas.put([key | CORE for key in keys], across)
        return both, across

    hold([0, SIDE], side_deltas)
    kept_far = swapped(kept_delta, "replica", far_mask)
    kept_near, beside_near = [gathered(piece, near_masks) for piece in side_deltas]
    keys = [mask for mask in kept_near if mask > 0]
    kept_near, beside_near = [kept_near[key] for key in keys], [beside_near[key] for key in keys]
    beside_own, *_ = lax.optimization_barrier((side_deltas[1], *kept_near))
    beside_far = swapped(beside_own, "replica", far_mask)
    all_here = [packed[0][0]] + [piece[0] for piece in arrived] + [crossed[0]] + [other[i] for i in range(len(arrived))]
    all_here, _ = lax.optimization_barrier((jnp.stack(all_here), side_deltas[1]))
    keys_beside = [4 * mask | SIDE for mask in [0] + others_of]
    rows.put(keys_beside + [key | CORE for key in keys_beside], swapped(all_here, "replica", SIDE))
    hold(keys + [key | SIDE for key in keys], kept_near + beside_near)
    far, _ = hold([far_mask, far_mask | SIDE], [kept_far, beside_far])
    far, *_ = lax.optimization_barrier((far, *kept_near, *beside_near))
    for key, piece in gathered(far, near_masks).items():
        if key > 0:
            keys = [far_mask | key, far_mask | key | SIDE]
            deltas.put(keys, piece)
            deltas.put([key | CORE for key in keys], swapped(piece, "replica", CORE))

    products = gram(where, rows, deltas, replicas)
    products = products + swapped(products, "replica", CORE)
    mask = 4
    while mask < replicas:
        products = products + swapped(products, "replica", mask)
        mask *= 2
    kept_block, sent_block = combine(where, products, rows, deltas)
    other_block = swapped(sent_block, "replica", SIDE)
    combined = jnp.where(
        side == 0, jnp.stack([kept_block, other_block]), jnp.stack([other_block, kept_block])
    )
    new_weight, moment_one, moment_two = adam_update(
        combined, weights[0], first_moment[0], second_moment[0]
    )
    return (new_weight[None], moment_one[None], moment_two[None])


def solution(mesh):
    in_specs = (
        P("replica", "expert", None),
        P(None, "replica", None),
        P("expert", "replica"),
        P("expert", "replica", None, None),
        P("expert", None, "replica", None),
        P("expert", None, "replica", None),
        P("expert", None, "replica", None),
    )
    out_specs = (
        P("expert", None, "replica", None),
        P("expert", None, "replica", None),
        P("expert", None, "replica", None),
    )
    return jax.shard_map(shards, mesh=mesh, in_specs=in_specs, out_specs=out_specs, check_vma=False)
```

profile of v0, /device:TPU:0, one launch (start us, length us, event | category | flops | bytes accessed | tf_op | source)
XLA Modules:
  0.0 112.3 jit_solution(9416779844265515324)
XLA Ops:
  0.6 1.1 convert_bitcast_fusion.refs_5_
  1.7 3.1 %collective-permute-start.1 = (bf16[2,128,384]{2,1,0:T(8,128)(2,1)S(1)}, bf16[2,128,384]{2,1,0:T(8,128)(2,1)S(1)}, u32[]{:S(2)}, u32[]{:S(2)}) collective-permute-start(bf16[2,128,384]{2,1,0:T(8,128)(2,1)S(1)} %convert_bitcast_fusion.refs_5_), channel_id=1, source_target_pairs={{0,4},{1,5},{2,6},{3,7},{4,0},{5,1},{6,2},{7,3},{8,12},{9,13},{10,... | collective-permute-start | bytes 589832 | tf_op jit(solution)/shard_map/ppermute | solution.py:35
  4.8 2.6 %collective-permute-start = (bf16[2,128,384]{2,1,0:T(8,128)(2,1)S(1)}, bf16[2,128,384]{2,1,0:T(8,128)(2,1)S(1)}, u32[]{:S(2)}, u32[]{:S(2)}) collective-permute-start(bf16[2,128,384]{2,1,0:T(8,128)(2,1)S(1)} %convert_bitcast_fusion.refs_5_), channel_id=1, source_target_pairs={{0,8},{1,9},{2,10},{3,11},{4,12},{5,13},{6,14},{7,15},{8,0},{9,1},... | collective-permute-start | bytes 589832 | tf_op jit(solution)/shard_map/ppermute | solution.py:35
  7.4 0.7 copy.12
  8.1 0.1 stack.94.where_ref
  8.2 1.2 %row_picks.1.pick_ref = bf16[448,2048]{1,0:T(8,128)(2,1)S(1)} custom-call(s32[6]{0:T(128)S(1)} %stack.94.where_ref, s32[2,256]{1,0:T(2,128)S(1)} %bitcast.30), custom_call_target="tpu_custom_call" | custom-call | flops 1 | bytes 1 | tf_op jit(solution)/shard_map/row_picks/pallas_call | solution.py:117
  9.4 4.5 %listed_rows.2 = (bf16[1,192,1024]{2,1,0:T(8,128)(2,1)S(1)}, bf16[256,1024]{1,0:T(8,128)(2,1)S(1)}) custom-call(s32[6]{0:T(128)S(1)} %stack.94.where_ref, bf16[448,2048]{1,0:T(8,128)(2,1)S(1)} %row_picks.1.pick_ref, bf16[2048,2048]{1,0:T(8,128)(2,1)} %bitcast.33), custom_call_target="tpu_custom_call" | custom-call | flops 1 | bytes 1 | tf_op jit(solution)/shard_map/listed_rows/pallas_call | solution.py:141
  13.9 1.6 %collective-permute-start.4 = (bf16[1,192,1024]{2,1,0:T(8,128)(2,1)S(1)}, bf16[1,192,1024]{2,1,0:T(8,128)(2,1)S(1)}, u32[]{:S(2)}, u32[]{:S(2)}) collective-permute-start(bf16[1,192,1024]{2,1,0:T(8,128)(2,1)S(1)} %get-tuple-element.32), channel_id=1, source_target_pairs={{0,16},{16,0},{1,17},{17,1},{2,18},{18,2},{3,19},{19,3},{4,20},{20... | collective-permute-start | bytes 1179656 | tf_op jit(solution)/shard_map/ppermute | solution.py:35
  15.6 0.8 collective-permute-done.refs_7_
  16.3 1.5 %collective-permute-start.2 = (bf16[2,2,128,384]{3,2,1,0:T(8,128)(2,1)S(1)}, bf16[2,2,128,384]{3,2,1,0:T(8,128)(2,1)S(1)}, u32[]{:S(2)}, u32[]{:S(2)}) collective-permute-start(bf16[2,2,128,384]{3,2,1,0:T(8,128)(2,1)S(1)} %pad_maximum_fusion.1), channel_id=1, source_target_pairs={{0,2},{1,3},{2,0},{3,1},{4,6},{5,7},{6,4},{7,5},{8,10},{9,11},{10,... | collective-permute-start | bytes 1179656 | tf_op jit(solution)/shard_map/ppermute | solution.py:35
  17.9 4.5 %listed_rows.3 = (bf16[1,192,1024]{2,1,0:T(8,128)(2,1)S(1)}, bf16[256,1024]{1,0:T(8,128)(2,1)S(1)}) custom-call(s32[6]{0:T(128)S(1)} %stack.94.where_ref, bf16[448,2048]{1,0:T(8,128)(2,1)S(1)} %row_picks.1.pick_ref, bf16[2048,2048]{1,0:T(8,128)(2,1)} %bitcast.34), custom_call_target="tpu_custom_call" | custom-call | flops 1 | bytes 1 | tf_op jit(solution)/shard_map/listed_rows/pallas_call | solution.py:141
  22.4 1.6 %collective-permute-start.3 = (bf16[1,192,1024]{2,1,0:T(8,128)(2,1)S(1)}, bf16[1,192,1024]{2,1,0:T(8,128)(2,1)S(1)}, u32[]{:S(2)}, u32[]{:S(2)}) collective-permute-start(bf16[1,192,1024]{2,1,0:T(8,128)(2,1)S(1)} %get-tuple-element.29), channel_id=1, source_target_pairs={{0,16},{16,0},{1,17},{17,1},{2,18},{18,2},{3,19},{19,3},{4,20},{20... | collective-permute-start | bytes 1179656 | tf_op jit(solution)/shard_map/ppermute | solution.py:35
  23.9 0.4 collective-permute-start.10
  24.4 1.0 collective-permute-done.4.refs_0_
  25.4 1.0 merged_rows.3
  26.4 1.1 collective-permute-start.6
  27.5 1.1 collective-permute-start.5
  28.6 4.1 %collective-permute-done.3.refs_0_ = bf16[1,192,1024]{2,1,0:T(8,128)(2,1)S(1)} collective-permute-done((bf16[1,192,1024]{2,1,0:T(8,128)(2,1)S(1)}, bf16[1,192,1024]{2,1,0:T(8,128)(2,1)S(1)}, u32[]{:S(2)}, u32[]{:S(2)}) %collective-permute-start.3) | collective-permute-done | bytes 393248 | tf_op jit(solution)/shard_map/ppermute | solution.py:35
  32.7 1.0 merged_rows.2
  33.8 0.1 pad_maximum_fusion
  33.8 0.1 collective-permute-start.9
  33.9 0.1 collective-permute-done.10.refs_8_
  34.1 1.5 %collective-permute-start.11 = (bf16[2,2,128,384]{3,2,1,0:T(8,128)(2,1)S(1)}, bf16[2,2,128,384]{3,2,1,0:T(8,128)(2,1)S(1)}, u32[]{:S(2)}, u32[]{:S(2)}) collective-permute-start(bf16[2,2,128,384]{3,2,1,0:T(8,128)(2,1)S(1)} %pad_maximum_fusion.3), channel_id=1, source_target_pairs={{0,2},{1,3},{2,0},{3,1},{4,6},{5,7},{6,4},{7,5},{8,10},{9,11},{10,... | collective-permute-start | bytes 1179656 | tf_op jit(solution)/shard_map/ppermute | solution.py:35
  35.6 0.4 collective-permute-start.7
  36.0 12.8 %collective-permute-done.5.refs_1_ = bf16[2,2,256,128]{3,2,1,0:T(8,128)(2,1)S(1)} collective-permute-done((bf16[2,2,256,128]{3,2,1,0:T(8,128)(2,1)S(1)}, bf16[2,2,256,128]{3,2,1,0:T(8,128)(2,1)S(1)}, u32[]{:S(2)}, u32[]{:S(2)}) %collective-permute-start.5) | collective-permute-done | bytes 262176 | tf_op jit(solution)/shard_map/ppermute | solution.py:35
  48.8 0.0 collective-permute-done.6.refs_2_
  48.9 0.0 collective-permute-done.11.refs_10_
  48.9 0.0 collective-permute-done.9.refs_4_.refs_5_
  48.9 2.3 %forward_values.1 = (f32[256,384]{1,0:T(8,128)S(1)}, f32[256,384]{1,0:T(8,128)S(1)}, f32[256,384]{1,0:T(8,128)S(1)}, f32[256,384]{1,0:T(8,128)S(1)}) custom-call(s32[6]{0:T(128)S(1)} %stack.94.where_ref, bf16[2,2,256,128]{3,2,1,0:T(8,128)(2,1)S(1)} %get-tuple-element.30.refs_0_, bf16[2,2,256,128]{3,2,1,0:T(8,128)(2,1)S(1)} %get-tuple-element.35.refs_1_, ...), custom_call_target="tpu_custom_call" | custom-call | flops 1 | bytes 1 | tf_op jit(solution)/shard_map/forward_values/pallas_call | solution.py:217
  51.2 0.1 collective-permute-start.12
  51.3 0.5 collective-permute-start.13
  51.8 0.0 collective-permute-done.7.refs_3_
  51.9 0.1 collective-permute-start.8
  52.7 0.3 collective-permute-done.12.gate_other_ref
  53.0 0.6 collective-permute-done.13.up_other_ref
  53.6 0.8 deltas.1
  54.4 1.5 %collective-permute-start.14 = (bf16[256,384]{1,0:T(8,128)(2,1)S(1)}, bf16[256,384]{1,0:T(8,128)(2,1)S(1)}, u32[]{:S(2)}, u32[]{:S(2)}) collective-permute-start(bf16[256,384]{1,0:T(8,128)(2,1)S(1)} %get-tuple-element.40), channel_id=1, source_target_pairs={{0,2},{1,3},{2,0},{3,1},{4,6},{5,7},{6,4},{7,5},{8,10},{9,11},{10,... | collective-permute-start | bytes 589832 | tf_op jit(solution)/shard_map/ppermute | solution.py:35
  55.9 2.0 %collective-permute-start.20 = (bf16[256,384]{1,0:T(8,128)(2,1)S(1)}, bf16[256,384]{1,0:T(8,128)(2,1)S(1)}, u32[]{:S(2)}, u32[]{:S(2)}) collective-permute-start(bf16[256,384]{1,0:T(8,128)(2,1)S(1)} %get-tuple-element.42), channel_id=1, source_target_pairs={{0,8},{1,9},{2,10},{3,11},{4,12},{5,13},{6,14},{7,15},{8,0},{9,1},... | collective-permute-start | bytes 589832 | tf_op jit(solution)/shard_map/ppermute | solution.py:35
  57.8 3.6 %collective-permute-done.14 = bf16[256,384]{1,0:T(8,128)(2,1)S(1)} collective-permute-done((bf16[256,384]{1,0:T(8,128)(2,1)S(1)}, bf16[256,384]{1,0:T(8,128)(2,1)S(1)}, u32[]{:S(2)}, u32[]{:S(2)}) %collective-permute-start.14) | collective-permute-done | bytes 196640 | tf_op jit(solution)/shard_map/ppermute | solution.py:35
  61.4 4.0 %collective-permute-done.17 = bf16[256,384]{1,0:T(8,128)(2,1)S(1)} collective-permute-done((bf16[256,384]{1,0:T(8,128)(2,1)S(1)}, bf16[256,384]{1,0:T(8,128)(2,1)S(1)}, u32[]{:S(2)}, u32[]{:S(2)}) %collective-permute-start.17) | collective-permute-done | bytes 196640 | tf_op jit(solution)/shard_map/ppermute | solution.py:35
  65.4 0.4 collective-permute-start.21
  65.8 0.1 constant_dynamic-update-slice_fusion
  65.9 0.6 collective-permute-start.15
  66.5 2.5 %collective-permute-start.18 = (bf16[256,384]{1,0:T(8,128)(2,1)S(1)}, bf16[256,384]{1,0:T(8,128)(2,1)S(1)}, u32[]{:S(2)}, u32[]{:S(2)}) collective-permute-start(bf16[256,384]{1,0:T(8,128)(2,1)S(1)} %collective-permute-done.14), channel_id=1, source_target_pairs={{0,4},{1,5},{2,6},{3,7},{4,0},{5,1},{6,2},{7,3},{8,12},{9,13},{10,... | collective-permute-start | bytes 589832 | tf_op jit(solution)/shard_map/ppermute | solution.py:35
  69.0 1.5 %collective-permute-done.20 = bf16[256,384]{1,0:T(8,128)(2,1)S(1)} collective-permute-done((bf16[256,384]{1,0:T(8,128)(2,1)S(1)}, bf16[256,384]{1,0:T(8,128)(2,1)S(1)}, u32[]{:S(2)}, u32[]{:S(2)}) %collective-permute-start.20) | collective-permute-done | bytes 196640 | tf_op jit(solution)/shard_map/ppermute | solution.py:35
  70.4 5.9 %collective-permute-done.21 = bf16[256,384]{1,0:T(8,128)(2,1)S(1)} collective-permute-done((bf16[256,384]{1,0:T(8,128)(2,1)S(1)}, bf16[256,384]{1,0:T(8,128)(2,1)S(1)}, u32[]{:S(2)}, u32[]{:S(2)}) %collective-permute-start.21) | collective-permute-done | bytes 196640 | tf_op jit(solution)/shard_map/ppermute | solution.py:35
  76.3 0.4 collective-permute-done.18
  76.8 0.1 collective-permute-start.16
  76.9 0.5 collective-permute-start.22
  77.4 0.1 collective-permute-start.19
  77.6 9.9 %collective-permute-done.23.refs_13_ = bf16[2,256,384]{2,1,0:T(8,128)(2,1)S(1)} collective-permute-done((bf16[2,256,384]{2,1,0:T(8,128)(2,1)S(1)}, bf16[2,256,384]{2,1,0:T(8,128)(2,1)S(1)}, u32[]{:S(2)}, u32[]{:S(2)}) %collective-permute-start.23) | collective-permute-done | bytes 393248 | tf_op jit(solution)/shard_map/ppermute | solution.py:35
  87.5 1.7 %collective-permute-done.24.refs_14_ = bf16[2,256,384]{2,1,0:T(8,128)(2,1)S(1)} collective-permute-done((bf16[2,256,384]{2,1,0:T(8,128)(2,1)S(1)}, bf16[2,256,384]{2,1,0:T(8,128)(2,1)S(1)}, u32[]{:S(2)}, u32[]{:S(2)}) %collective-permute-start.24) | collective-permute-done | bytes 393248 | tf_op jit(solution)/shard_map/ppermute | solution.py:35
  89.2 0.5 collective-permute-done.15.refs_6_
  89.7 3.4 %gradient_products.1 = f32[16,16]{1,0:T(8,128)S(1)} custom-call(s32[6]{0:T(128)S(1)} %stack.94.where_ref, bf16[2,2,256,128]{3,2,1,0:T(8,128)(2,1)S(1)} %get-tuple-element.30.refs_0_, bf16[2,2,256,128]{3,2,1,0:T(8,128)(2,1)S(1)} %collective-permute-done.5.refs_1_, bf16[2,2,256,128]{3,2,1,0:T(8,128)(2,1)S(1)} %collective-permute-done.6.refs_2_, ...), custom_call_target="tpu_custom_call" | custom-call | flops 1 | bytes 1 | tf_op jit(solution)/shard_map/gradient_products/pallas_call | solution.py:327
  93.1 0.1 collective-permute-start.25
  93.2 1.2 %collective-permute-done.25 = f32[16,16]{1,0:T(8,128)S(1)} collective-permute-done((f32[16,16]{1,0:T(8,128)S(1)}, f32[16,16]{1,0:T(8,128)S(1)}, u32[]{:S(2)}, u32[]{:S(2)}) %collective-permute-start.25) | collective-permute-done | bytes 1056 | tf_op jit(solution)/shard_map/ppermute | solution.py:35
  94.3 2.5 %collective-permute-start.26 = (f32[16,16]{1,0:T(8,128)S(1)}, f32[16,16]{1,0:T(8,128)S(1)}, u32[]{:S(2)}, u32[]{:S(2)}) collective-permute-start(f32[16,16]{1,0:T(8,128)S(1)} %add.31), channel_id=1, source_target_pairs={{0,4},{1,5},{2,6},{3,7},{4,0},{5,1},{6,2},{7,3},{8,12},{9,13},{10,... | collective-permute-start | bytes 3080 | tf_op jit(solution)/shard_map/ppermute | solution.py:35
  96.8 1.6 %collective-permute-done.26 = f32[16,16]{1,0:T(8,128)S(1)} collective-permute-done((f32[16,16]{1,0:T(8,128)S(1)}, f32[16,16]{1,0:T(8,128)S(1)}, u32[]{:S(2)}, u32[]{:S(2)}) %collective-permute-start.26) | collective-permute-done | bytes 1056 | tf_op jit(solution)/shard_map/ppermute | solution.py:35
  98.4 2.1 %collective-permute-start.27 = (f32[16,16]{1,0:T(8,128)S(1)}, f32[16,16]{1,0:T(8,128)S(1)}, u32[]{:S(2)}, u32[]{:S(2)}) collective-permute-start(f32[16,16]{1,0:T(8,128)S(1)} %add.32), channel_id=1, source_target_pairs={{0,8},{1,9},{2,10},{3,11},{4,12},{5,13},{6,14},{7,15},{8,0},{9,1},... | collective-permute-start | bytes 3080 | tf_op jit(solution)/shard_map/ppermute | solution.py:35
  100.5 2.5 %collective-permute-done.27 = f32[16,16]{1,0:T(8,128)S(1)} collective-permute-done((f32[16,16]{1,0:T(8,128)S(1)}, f32[16,16]{1,0:T(8,128)S(1)}, u32[]{:S(2)}, u32[]{:S(2)}) %collective-permute-start.27) | collective-permute-done | bytes 1056 | tf_op jit(solution)/shard_map/ppermute | solution.py:35
  103.0 2.3 %combined_gradient.1 = (f32[128,384]{1,0:T(8,128)S(1)}, f32[128,384]{1,0:T(8,128)S(1)}) custom-call(s32[6]{0:T(128)S(1)} %stack.94.where_ref, f32[16,16]{1,0:T(8,128)S(1)} %add.33.gram_ref, bf16[2,2,256,128]{3,2,1,0:T(8,128)(2,1)S(1)} %get-tuple-element.30.refs_0_, bf16[2,2,256,128]{3,2,1,0:T(8,128)(2,1)S(1)} %collective-permute-done.5.refs_1_, ...), custom_call_target="tpu_custom_call" | custom-call | flops 1 | bytes 1 | tf_op jit(solution)/shard_map/combined_gradient/pallas_call | solution.py:376
  105.3 0.6 collective-permute-start.28
  105.9 5.2 %collective-permute-done.28 = f32[128,384]{1,0:T(8,128)S(1)} collective-permute-done((f32[128,384]{1,0:T(8,128)S(1)}, f32[128,384]{1,0:T(8,128)S(1)}, u32[]{:S(2)}, u32[]{:S(2)}) %collective-permute-start.28) | collective-permute-done | bytes 196640 | tf_op jit(solution)/shard_map/ppermute | solution.py:35
  111.1 1.2 %multiply_subtract_fusion = (f32[1,2,128,384]{3,2,1,0:T(8,128)}, f32[1,2,128,384]{3,2,1,0:T(8,128)}, f32[1,2,128,384]{3,2,1,0:T(8,128)}) fusion(f32[1,2,128,384]{3,2,1,0:T(8,128)S(1)} %copy-done.1, f32[1,1,128,384]{3,2,1,0:T(8,128)S(1)} %bitcast.28, f32[1,1,128,384]{3,2,1,0:T(8,128)S(1)} %bitcast.35, pred[]{:T(512)S(6)} %eq.3, ...), kind=kLoop, calls=%fused_computation.10 | loop fusion | flops 1769472 | bytes 2752513 | tf_op jit(solution)/shard_map/sub | solution.py:59
  (35 shorter events, 0.5 us)
Async XLA Ops:
  0.6 14.9 %copy-start.1 = (f32[1,2,128,384]{3,2,1,0:T(8,128)S(1)}, f32[1,2,128,384]{3,2,1,0:T(8,128)}, u32[]{:S(2)}) copy-start(f32[1,2,128,384]{3,2,1,0:T(8,128)} %param.11) | copy-start | bytes 1179652
  1.7 13.8 %collective-permute-start.1 = (bf16[2,128,384]{2,1,0:T(8,128)(2,1)S(1)}, bf16[2,128,384]{2,1,0:T(8,128)(2,1)S(1)}, u32[]{:S(2)}, u32[]{:S(2)}) collective-permute-start(bf16[2,128,384]{2,1,0:T(8,128)(2,1)S(1)} %convert_bitcast_fusion.refs_5_), channel_id=1, source_target_pairs={{0,4},{1,5},{2,6},{3,7},{4,0},{5,1},{6,2},{7,3},{8,12},{9,13},{10,... | collective-permute-start | bytes 589832 | tf_op jit(solution)/shard_map/ppermute | solution.py:35
  4.8 11.5 %collective-permute-start = (bf16[2,128,384]{2,1,0:T(8,128)(2,1)S(1)}, bf16[2,128,384]{2,1,0:T(8,128)(2,1)S(1)}, u32[]{:S(2)}, u32[]{:S(2)}) collective-permute-start(bf16[2,128,384]{2,1,0:T(8,128)(2,1)S(1)} %convert_bitcast_fusion.refs_5_), channel_id=1, source_target_pairs={{0,8},{1,9},{2,10},{3,11},{4,12},{5,13},{6,14},{7,15},{8,0},{9,1},... | collective-permute-start | bytes 589832 | tf_op jit(solution)/shard_map/ppermute | solution.py:35
  13.9 11.5 %collective-permute-start.4 = (bf16[1,192,1024]{2,1,0:T(8,128)(2,1)S(1)}, bf16[1,192,1024]{2,1,0:T(8,128)(2,1)S(1)}, u32[]{:S(2)}, u32[]{:S(2)}) collective-permute-start(bf16[1,192,1024]{2,1,0:T(8,128)(2,1)S(1)} %get-tuple-element.32), channel_id=1, source_target_pairs={{0,16},{16,0},{1,17},{17,1},{2,18},{18,2},{3,19},{19,3},{4,20},{20... | collective-permute-start | bytes 1179656 | tf_op jit(solution)/shard_map/ppermute | solution.py:35
  16.3 37.2 %copy-start = (bf16[1,1,256,384]{3,2,1,0:T(8,128)(2,1)S(1)}, bf16[1,1,256,384]{3,2,1,0:T(8,128)(2,1)}, u32[]{:S(2)}) copy-start(bf16[1,1,256,384]{3,2,1,0:T(8,128)(2,1)} %param.10) | copy-start | bytes 589828
  16.3 12.3 %collective-permute-start.2 = (bf16[2,2,128,384]{3,2,1,0:T(8,128)(2,1)S(1)}, bf16[2,2,128,384]{3,2,1,0:T(8,128)(2,1)S(1)}, u32[]{:S(2)}, u32[]{:S(2)}) collective-permute-start(bf16[2,2,128,384]{3,2,1,0:T(8,128)(2,1)S(1)} %pad_maximum_fusion.1), channel_id=1, source_target_pairs={{0,2},{1,3},{2,0},{3,1},{4,6},{5,7},{6,4},{7,5},{8,10},{9,11},{10,... | collective-permute-start | bytes 1179656 | tf_op jit(solution)/shard_map/ppermute | solution.py:35
  22.4 10.3 %collective-permute-start.3 = (bf16[1,192,1024]{2,1,0:T(8,128)(2,1)S(1)}, bf16[1,192,1024]{2,1,0:T(8,128)(2,1)S(1)}, u32[]{:S(2)}, u32[]{:S(2)}) collective-permute-start(bf16[1,192,1024]{2,1,0:T(8,128)(2,1)S(1)} %get-tuple-element.29), channel_id=1, source_target_pairs={{0,16},{16,0},{1,17},{17,1},{2,18},{18,2},{3,19},{19,3},{4,20},{20... | collective-permute-start | bytes 1179656 | tf_op jit(solution)/shard_map/ppermute | solution.py:35
  23.9 10.1 %collective-permute-start.10 = (bf16[2,128,384]{2,1,0:T(8,128)(2,1)S(1)}, bf16[2,128,384]{2,1,0:T(8,128)(2,1)S(1)}, u32[]{:S(2)}, u32[]{:S(2)}) collective-permute-start(bf16[2,128,384]{2,1,0:T(8,128)(2,1)S(1)} %collective-permute-done.refs_7_), channel_id=1, source_target_pairs={{0,4},{1,5},{2,6},{3,7},{4,0},{5,1},{6,2},{7,3},{8,12},{9,13},{10,... | collective-permute-start | bytes 589832 | tf_op jit(solution)/shard_map/ppermute | solution.py:35
  26.4 22.4 %collective-permute-start.6 = (bf16[2,2,256,128]{3,2,1,0:T(8,128)(2,1)S(1)}, bf16[2,2,256,128]{3,2,1,0:T(8,128)(2,1)S(1)}, u32[]{:S(2)}, u32[]{:S(2)}) collective-permute-start(bf16[2,2,256,128]{3,2,1,0:T(8,128)(2,1)S(1)} %get-tuple-element.34.refs_3_), channel_id=1, source_target_pairs={{0,12},{1,13},{2,14},{3,15},{4,8},{5,9},{6,10},{7,11},{8,4},{9,5},... | collective-permute-start | bytes 786440 | tf_op jit(solution)/shard_map/ppermute | solution.py:35
  27.5 21.3 %collective-permute-start.5 = (bf16[2,2,256,128]{3,2,1,0:T(8,128)(2,1)S(1)}, bf16[2,2,256,128]{3,2,1,0:T(8,128)(2,1)S(1)}, u32[]{:S(2)}, u32[]{:S(2)}) collective-permute-start(bf16[2,2,256,128]{3,2,1,0:T(8,128)(2,1)S(1)} %get-tuple-element.33.refs_2_), channel_id=1, source_target_pairs={{0,8},{1,9},{2,10},{3,11},{4,12},{5,13},{6,14},{7,15},{8,0},{9,1},... | collective-permute-start | bytes 786440 | tf_op jit(solution)/shard_map/ppermute | solution.py:35
  33.8 15.0 %collective-permute-start.9 = (bf16[4,2,256,128]{3,2,1,0:T(8,128)(2,1)S(1)}, bf16[4,2,256,128]{3,2,1,0:T(8,128)(2,1)S(1)}, u32[]{:S(2)}, u32[]{:S(2)}) collective-permute-start(bf16[4,2,256,128]{3,2,1,0:T(8,128)(2,1)S(1)} %pad_maximum_fusion), channel_id=1, source_target_pairs={{0,1},{1,0},{2,3},{3,2},{4,5},{5,4},{6,7},{7,6},{8,9},{9,8},{10,11... | collective-permute-start | bytes 1572872 | tf_op jit(solution)/shard_map/ppermute | solution.py:35
  34.1 14.8 %collective-permute-start.11 = (bf16[2,2,128,384]{3,2,1,0:T(8,128)(2,1)S(1)}, bf16[2,2,128,384]{3,2,1,0:T(8,128)(2,1)S(1)}, u32[]{:S(2)}, u32[]{:S(2)}) collective-permute-start(bf16[2,2,128,384]{3,2,1,0:T(8,128)(2,1)S(1)} %pad_maximum_fusion.3), channel_id=1, source_target_pairs={{0,2},{1,3},{2,0},{3,1},{4,6},{5,7},{6,4},{7,5},{8,10},{9,11},{10,... | collective-permute-start | bytes 1179656 | tf_op jit(solution)/shard_map/ppermute | solution.py:35
  35.6 16.2 %collective-permute-start.7 = (bf16[2,2,256,128]{3,2,1,0:T(8,128)(2,1)S(1)}, bf16[2,2,256,128]{3,2,1,0:T(8,128)(2,1)S(1)}, u32[]{:S(2)}, u32[]{:S(2)}) collective-permute-start(bf16[2,2,256,128]{3,2,1,0:T(8,128)(2,1)S(1)} %get-tuple-element.35.refs_1_), channel_id=1, source_target_pairs={{0,4},{1,5},{2,6},{3,7},{4,0},{5,1},{6,2},{7,3},{8,12},{9,13},{10,... | collective-permute-start | bytes 786440 | tf_op jit(solution)/shard_map/ppermute | solution.py:35
  51.2 1.8 %collective-permute-start.12 = (f32[256,384]{1,0:T(8,128)S(1)}, f32[256,384]{1,0:T(8,128)S(1)}, u32[]{:S(2)}, u32[]{:S(2)}) collective-permute-start(f32[256,384]{1,0:T(8,128)S(1)} %get-tuple-element.38), channel_id=1, source_target_pairs={{0,1},{1,0},{2,3},{3,2},{4,5},{5,4},{6,7},{7,6},{8,9},{9,8},{10,11... | collective-permute-start | bytes 1179656 | tf_op jit(solution)/shard_map/ppermute | solution.py:35
  51.3 2.3 %collective-permute-start.13 = (f32[256,384]{1,0:T(8,128)S(1)}, f32[256,384]{1,0:T(8,128)S(1)}, u32[]{:S(2)}, u32[]{:S(2)}) collective-permute-start(f32[256,384]{1,0:T(8,128)S(1)} %get-tuple-element.39), channel_id=1, source_target_pairs={{0,1},{1,0},{2,3},{3,2},{4,5},{5,4},{6,7},{7,6},{8,9},{9,8},{10,11... | collective-permute-start | bytes 1179656 | tf_op jit(solution)/shard_map/ppermute | solution.py:35
  51.9 14.0 %collective-permute-start.8 = (bf16[3,2,256,128]{3,2,1,0:T(8,128)(2,1)S(1)}, bf16[3,2,256,128]{3,2,1,0:T(8,128)(2,1)S(1)}, u32[]{:S(2)}, u32[]{:S(2)}) collective-permute-start(bf16[3,2,256,128]{3,2,1,0:T(8,128)(2,1)S(1)} %pad_maximum_fusion.2), channel_id=1, source_target_pairs={{0,1},{1,0},{2,3},{3,2},{4,5},{5,4},{6,7},{7,6},{8,9},{9,8},{10,11... | collective-permute-start | bytes 1179656 | tf_op jit(solution)/shard_map/ppermute | solution.py:35
  53.5 57.5 %copy-start.2 = (f32[1,2,128,384]{3,2,1,0:T(8,128)S(1)}, f32[1,2,128,384]{3,2,1,0:T(8,128)}, u32[]{:S(2)}) copy-start(f32[1,2,128,384]{3,2,1,0:T(8,128)} %param.12) | copy-start | bytes 1179652
  53.5 57.5 %copy-start.3 = (f32[1,2,128,384]{3,2,1,0:T(8,128)S(1)}, f32[1,2,128,384]{3,2,1,0:T(8,128)}, u32[]{:S(2)}) copy-start(f32[1,2,128,384]{3,2,1,0:T(8,128)} %param.13) | copy-start | bytes 1179652
  54.4 7.0 %collective-permute-start.14 = (bf16[256,384]{1,0:T(8,128)(2,1)S(1)}, bf16[256,384]{1,0:T(8,128)(2,1)S(1)}, u32[]{:S(2)}, u32[]{:S(2)}) collective-permute-start(bf16[256,384]{1,0:T(8,128)(2,1)S(1)} %get-tuple-element.40), channel_id=1, source_target_pairs={{0,2},{1,3},{2,0},{3,1},{4,6},{5,7},{6,4},{7,5},{8,10},{9,11},{10,... | collective-permute-start | bytes 589832 | tf_op jit(solution)/shard_map/ppermute | solution.py:35
  55.9 9.5 %collective-permute-start.17 = (bf16[256,384]{1,0:T(8,128)(2,1)S(1)}, bf16[256,384]{1,0:T(8,128)(2,1)S(1)}, u32[]{:S(2)}, u32[]{:S(2)}) collective-permute-start(bf16[256,384]{1,0:T(8,128)(2,1)S(1)} %get-tuple-element.42), channel_id=1, source_target_pairs={{0,4},{1,5},{2,6},{3,7},{4,0},{5,1},{6,2},{7,3},{8,12},{9,13},{10,... | collective-permute-start | bytes 589832 | tf_op jit(solution)/shard_map/ppermute | solution.py:35
  55.9 14.5 %collective-permute-start.20 = (bf16[256,384]{1,0:T(8,128)(2,1)S(1)}, bf16[256,384]{1,0:T(8,128)(2,1)S(1)}, u32[]{:S(2)}, u32[]{:S(2)}) collective-permute-start(bf16[256,384]{1,0:T(8,128)(2,1)S(1)} %get-tuple-element.42), channel_id=1, source_target_pairs={{0,8},{1,9},{2,10},{3,11},{4,12},{5,13},{6,14},{7,15},{8,0},{9,1},... | collective-permute-start | bytes 589832 | tf_op jit(solution)/shard_map/ppermute | solution.py:35
  65.4 10.9 %collective-permute-start.21 = (bf16[256,384]{1,0:T(8,128)(2,1)S(1)}, bf16[256,384]{1,0:T(8,128)(2,1)S(1)}, u32[]{:S(2)}, u32[]{:S(2)}) collective-permute-start(bf16[256,384]{1,0:T(8,128)(2,1)S(1)} %collective-permute-done.14), channel_id=1, source_target_pairs={{0,8},{1,9},{2,10},{3,11},{4,12},{5,13},{6,14},{7,15},{8,0},{9,1},... | collective-permute-start | bytes 589832 | tf_op jit(solution)/shard_map/ppermute | solution.py:35
  65.9 23.8 %collective-permute-start.15 = (bf16[8,2,256,128]{3,2,1,0:T(8,128)(2,1)S(1)}, bf16[8,2,256,128]{3,2,1,0:T(8,128)(2,1)S(1)}, u32[]{:S(2)}, u32[]{:S(2)}) collective-permute-start(bf16[8,2,256,128]{3,2,1,0:T(8,128)(2,1)S(1)} %constant_dynamic-update-slice_fusion), channel_id=1, source_target_pairs={{0,2},{1,3},{2,0},{3,1},{4,6},{5,7},{6,4},{7,5},{8,10},{9,11},{10,... | collective-permute-start | bytes 3145736 | tf_op jit(solution)/shard_map/ppermute | solution.py:35
  66.5 10.3 %collective-permute-start.18 = (bf16[256,384]{1,0:T(8,128)(2,1)S(1)}, bf16[256,384]{1,0:T(8,128)(2,1)S(1)}, u32[]{:S(2)}, u32[]{:S(2)}) collective-permute-start(bf16[256,384]{1,0:T(8,128)(2,1)S(1)} %collective-permute-done.14), channel_id=1, source_target_pairs={{0,4},{1,5},{2,6},{3,7},{4,0},{5,1},{6,2},{7,3},{8,12},{9,13},{10,... | collective-permute-start | bytes 589832 | tf_op jit(solution)/shard_map/ppermute | solution.py:35
  76.8 10.7 %collective-permute-start.23 = (bf16[2,256,384]{2,1,0:T(8,128)(2,1)S(1)}, bf16[2,256,384]{2,1,0:T(8,128)(2,1)S(1)}, u32[]{:S(2)}, u32[]{:S(2)}) collective-permute-start(bf16[2,256,384]{2,1,0:T(8,128)(2,1)S(1)} %pad_maximum_fusion.6.refs_11_), channel_id=1, source_target_pairs={{0,4},{1,5},{2,6},{3,7},{4,0},{5,1},{6,2},{7,3},{8,12},{9,13},{10,... | collective-permute-start | bytes 1179656 | tf_op jit(solution)/shard_map/ppermute | solution.py:35
  76.8 10.7 %collective-permute-start.16 = (bf16[2,256,384]{2,1,0:T(8,128)(2,1)S(1)}, bf16[2,256,384]{2,1,0:T(8,128)(2,1)S(1)}, u32[]{:S(2)}, u32[]{:S(2)}) collective-permute-start(bf16[2,256,384]{2,1,0:T(8,128)(2,1)S(1)} %pad_maximum_fusion.4.refs_7_), channel_id=1, source_target_pairs={{0,1},{1,0},{2,3},{3,2},{4,5},{5,4},{6,7},{7,6},{8,9},{9,8},{10,11... | collective-permute-start | bytes 1179656 | tf_op jit(solution)/shard_map/ppermute | solution.py:35
  76.9 10.6 %collective-permute-start.22 = (bf16[2,256,384]{2,1,0:T(8,128)(2,1)S(1)}, bf16[2,256,384]{2,1,0:T(8,128)(2,1)S(1)}, u32[]{:S(2)}, u32[]{:S(2)}) collective-permute-start(bf16[2,256,384]{2,1,0:T(8,128)(2,1)S(1)} %pad_maximum_fusion.6.refs_11_), channel_id=1, source_target_pairs={{0,1},{1,0},{2,3},{3,2},{4,5},{5,4},{6,7},{7,6},{8,9},{9,8},{10,11... | collective-permute-start | bytes 1179656 | tf_op jit(solution)/shard_map/ppermute | solution.py:35
  77.4 10.0 %collective-permute-start.19 = (bf16[2,256,384]{2,1,0:T(8,128)(2,1)S(1)}, bf16[2,256,384]{2,1,0:T(8,128)(2,1)S(1)}, u32[]{:S(2)}, u32[]{:S(2)}) collective-permute-start(bf16[2,256,384]{2,1,0:T(8,128)(2,1)S(1)} %pad_maximum_fusion.5.refs_9_), channel_id=1, source_target_pairs={{0,1},{1,0},{2,3},{3,2},{4,5},{5,4},{6,7},{7,6},{8,9},{9,8},{10,11... | collective-permute-start | bytes 1179656 | tf_op jit(solution)/shard_map/ppermute | solution.py:35
  87.5 1.7 %collective-permute-start.24 = (bf16[2,256,384]{2,1,0:T(8,128)(2,1)S(1)}, bf16[2,256,384]{2,1,0:T(8,128)(2,1)S(1)}, u32[]{:S(2)}, u32[]{:S(2)}) collective-permute-start(bf16[2,256,384]{2,1,0:T(8,128)(2,1)S(1)} %collective-permute-done.23.refs_13_), channel_id=1, source_target_pairs={{0,1},{1,0},{2,3},{3,2},{4,5},{5,4},{6,7},{7,6},{8,9},{9,8},{10,11... | collective-permute-start | bytes 1179656 | tf_op jit(solution)/shard_map/ppermute | solution.py:35
  93.1 1.2 %collective-permute-start.25 = (f32[16,16]{1,0:T(8,128)S(1)}, f32[16,16]{1,0:T(8,128)S(1)}, u32[]{:S(2)}, u32[]{:S(2)}) collective-permute-start(f32[16,16]{1,0:T(8,128)S(1)} %gradient_products.1), channel_id=1, source_target_pairs={{0,1},{1,0},{2,3},{3,2},{4,5},{5,4},{6,7},{7,6},{8,9},{9,8},{10,11... | collective-permute-start | bytes 3080 | tf_op jit(solution)/shard_map/ppermute | solution.py:35
  94.3 4.1 %collective-permute-start.26 = (f32[16,16]{1,0:T(8,128)S(1)}, f32[16,16]{1,0:T(8,128)S(1)}, u32[]{:S(2)}, u32[]{:S(2)}) collective-permute-start(f32[16,16]{1,0:T(8,128)S(1)} %add.31), channel_id=1, source_target_pairs={{0,4},{1,5},{2,6},{3,7},{4,0},{5,1},{6,2},{7,3},{8,12},{9,13},{10,... | collective-permute-start | bytes 3080 | tf_op jit(solution)/shard_map/ppermute | solution.py:35
  98.4 4.5 %collective-permute-start.27 = (f32[16,16]{1,0:T(8,128)S(1)}, f32[16,16]{1,0:T(8,128)S(1)}, u32[]{:S(2)}, u32[]{:S(2)}) collective-permute-start(f32[16,16]{1,0:T(8,128)S(1)} %add.32), channel_id=1, source_target_pairs={{0,8},{1,9},{2,10},{3,11},{4,12},{5,13},{6,14},{7,15},{8,0},{9,1},... | collective-permute-start | bytes 3080 | tf_op jit(solution)/shard_map/ppermute | solution.py:35
  105.3 5.7 %collective-permute-start.28 = (f32[128,384]{1,0:T(8,128)S(1)}, f32[128,384]{1,0:T(8,128)S(1)}, u32[]{:S(2)}, u32[]{:S(2)}) collective-permute-start(f32[128,384]{1,0:T(8,128)S(1)} %get-tuple-element.46), channel_id=1, source_target_pairs={{0,2},{1,3},{2,0},{3,1},{4,6},{5,7},{6,4},{7,5},{8,10},{9,11},{10,... | collective-permute-start | bytes 589832 | tf_op jit(solution)/shard_map/ppermute | solution.py:35
where the time goes:
time: 112 us
  waiting for transfers between devices  57.5 us (51%)
  starting transfers between devices  28.5 us (25%)
  Pallas kernels  21.1 us (19%)
  other arithmetic  2.68 us (2%)
  between operations  1.54 us (1%)
    ppermute x29, waiting for transfers between devices, swapped(): lax.ppermute(x, axis, [(i, i ^ mask) for i in range(lax.axis_size(axis))])  57.5 us
    ppermute x29, starting transfers between devices, swapped(): lax.ppermute(x, axis, [(i, i ^ mask) for i in range(lax.axis_size(axis))])  28.5 us
    pallas_call x2, Pallas kernels, listed_rows(): pl.pallas_call(functools.partial(listed_kernel, experts, most), out_shape...  9.04 us
    pallas_call x1, Pallas kernels, gram(): pl.pallas_call(functools.partial(gram_kernel, replicas, (rows, deltas)),...  3.35 us
    pallas_call x1, Pallas kernels, combine(): pl.pallas_call(functools.partial(combine_kernel, replicas, (rows, deltas)...  2.33 us
    pallas_call x1, Pallas kernels, forward(): pl.pallas_call(functools.partial(forward_kernel, uppers, blocks), out_sha...  2.31 us
  transfers between devices with their start and end apart: 29, of which 19 were waited for; matrix products, arithmetic and copies ran while one was open for 1% of the time, Pallas kernels for 14%

commit v1 on v0

--- a/solution.py
+++ b/solution.py
@@ -358,26 +358,26 @@
     return weights
 
 
-def combine_kernel(replicas, pieces, where_ref, gram_ref, *refs):
-    rows, deltas, (kept_ref, sent_ref, weight_ref) = split_refs(*pieces, refs)
+def combine_kernel(replicas, pieces, sent, where_ref, gram_ref, *refs):
+    rows, deltas, (out_ref, weight_ref) = split_refs(*pieces, refs)
     side, me = where_ref[4], where_ref[5]
     weight_ref[...] = jnp.broadcast_to(tree_weights(gram_ref[...], replicas), weight_ref.shape)
-    for ref, part in ((kept_ref, side), (sent_ref, 1 - side)):
-        total = jnp.zeros(ref.shape, f32)
-        for mask in range(replicas):
-            gradient = token_contract(rows(mask)[part], deltas(mask))
-            total = total + weight_ref[pl.ds(me ^ mask, 1), 0:1] * gradient
-        ref[...] = total
-
-
-def combine(where, products, rows, deltas):
+    part = 1 - side if sent else side
+    total = jnp.zeros(out_ref.shape, f32)
+    for mask in range(replicas):
+        gradient = token_contract(rows(mask)[part], deltas(mask))
+        total = total + weight_ref[pl.ds(me ^ mask, 1), 0:1] * gradient
+    out_ref[...] = total
+
+
+def combine(where, products, rows, deltas, sent):
     replicas = products.shape[0]
     out = jax.ShapeDtypeStruct((rows.arrays[0].shape[-1], deltas.arrays[0].shape[-1]), f32)
     return pl.pallas_call(
-        functools.partial(combine_kernel, replicas, (rows, deltas)),
-        out_shape=[out, out],
+        functools.partial(combine_kernel, replicas, (rows, deltas), sent),
+        out_shape=out,
         in_specs=[smem(), vmem()] + [vmem()] * (len(rows.arrays) + len(deltas.arrays)),
-        out_specs=[vmem()] * 2,
+        out_specs=vmem(),
         scratch_shapes=[pltpu.VMEM((replicas, 128), f32)],
         compiler_params=params(*rows.arrays, *deltas.arrays),
         cost_estimate=LIGHT,
@@ -475,8 +475,9 @@
     while mask < replicas:
         products = products + swapped(products, "replica", mask)
         mask *= 2
-    kept_block, sent_block = combine(where, products, rows, deltas)
+    sent_block = combine(where, products, rows, deltas, True)
     other_block = swapped(sent_block, "replica", SIDE)
+    kept_block = combine(where, products, rows, deltas, False)
     combined = jnp.where(
         side == 0, jnp.stack([kept_block, other_block]), jnp.stack([other_block, kept_block])
     )

time: 112 us -> 119 us (1.062)
  local copies, waits for them, and re-layouts: 0.98 us -> 8.84 us
  waiting for transfers between devices: 57.5 us -> 52.4 us
  Pallas kernels: 21.1 us -> 22.8 us
  other arithmetic: 2.68 us -> 4.09 us
    unnamed x14 -> x42, local copies, waits for them, and re-layouts: 0.82 us -> 8.68 us
    ppermute x29, waiting for transfers between devices: 57.5 us -> 52.4 us  [swapped(): lax.ppermute(x, axis, [(i, i ^ mask) for i in range(lax.axis_size(axis))])]
    pallas_call x1 -> x2, Pallas kernels: 2.33 us -> 4.1 us  [combine(): pl.pallas_call(functools.partial(combine_kernel, replicas, (rows, deltas)...]
    sub x1, other arithmetic: 1.21 us -> 2.62 us  [adam_update(): weight - learning_rate * (first_hat / (jnp.sqrt(second_hat) + adam_epsilo...]
  transfers between devices with their start and end apart: 29 -> 29, of which waited for: 19 -> 18; matrix products, arithmetic and copies ran while one was open for 1% -> 1% of each run, Pallas kernels for 14% -> 14%
where the time goes in v1:
time: 119 us; the launch traced here: 118 us
  waiting for transfers between devices  52.4 us (44%)
  starting transfers between devices  28.4 us (24%)
  Pallas kernels  22.8 us (19%)
  local copies, waits for them, and re-layouts  8.84 us (7%)
  other arithmetic  4.09 us (3%)
  between operations  1.64 us (1%)
    ppermute x29, waiting for transfers between devices, swapped(): lax.ppermute(x, axis, [(i, i ^ mask) for i in range(lax.axis_size(axis))])  52.4 us
    ppermute x29, starting transfers between devices, swapped(): lax.ppermute(x, axis, [(i, i ^ mask) for i in range(lax.axis_size(axis))])  28.4 us
    pallas_call x2, Pallas kernels, listed_rows(): pl.pallas_call(functools.partial(listed_kernel, experts, most), out_shape...  9.04 us
    unnamed x42, local copies, waits for them, and re-layouts  8.68 us
    pallas_call x2, Pallas kernels, combine(): pl.pallas_call(functools.partial(combine_kernel, replicas, (rows, deltas)...  4.1 us
    pallas_call x1, Pallas kernels, gram(): pl.pallas_call(functools.partial(gram_kernel, replicas, (rows, deltas)),...  3.33 us
    sub x1, other arithmetic, adam_update(): weight - learning_rate * (first_hat / (jnp.sqrt(second_hat) + adam_epsilo...  2.62 us
  transfers between devices with their start and end apart: 29, of which 18 were waited for; matrix products, arithmetic and copies ran while one was open for 1% of the time, Pallas kernels for 14%

profile of v1, /device:TPU:0, one launch (start us, length us, event | category | flops | bytes accessed | tf_op | source)
XLA Modules:
  0.0 118.2 jit_solution(1934413247987449573)
XLA Ops:
  0.6 1.1 convert_bitcast_fusion.refs_5_
  1.7 3.1 %collective-permute-start.1 = (bf16[2,128,384]{2,1,0:T(8,128)(2,1)S(1)}, bf16[2,128,384]{2,1,0:T(8,128)(2,1)S(1)}, u32[]{:S(2)}, u32[]{:S(2)}) collective-permute-start(bf16[2,128,384]{2,1,0:T(8,128)(2,1)S(1)} %convert_bitcast_fusion.refs_5_), channel_id=1, source_target_pairs={{0,4},{1,5},{2,6},{3,7},{4,0},{5,1},{6,2},{7,3},{8,12},{9,13},{10,... | collective-permute-start | bytes 589832 | tf_op jit(solution)/shard_map/ppermute | solution.py:35
  4.8 2.6 %collective-permute-start = (bf16[2,128,384]{2,1,0:T(8,128)(2,1)S(1)}, bf16[2,128,384]{2,1,0:T(8,128)(2,1)S(1)}, u32[]{:S(2)}, u32[]{:S(2)}) collective-permute-start(bf16[2,128,384]{2,1,0:T(8,128)(2,1)S(1)} %convert_bitcast_fusion.refs_5_), channel_id=1, source_target_pairs={{0,8},{1,9},{2,10},{3,11},{4,12},{5,13},{6,14},{7,15},{8,0},{9,1},... | collective-permute-start | bytes 589832 | tf_op jit(solution)/shard_map/ppermute | solution.py:35
  7.4 0.7 copy.12
  8.1 0.1 stack.94.where_ref
  8.2 1.2 %row_picks.1.pick_ref = bf16[448,2048]{1,0:T(8,128)(2,1)S(1)} custom-call(s32[6]{0:T(128)S(1)} %stack.94.where_ref, s32[2,256]{1,0:T(2,128)S(1)} %bitcast.30), custom_call_target="tpu_custom_call" | custom-call | flops 1 | bytes 1 | tf_op jit(solution)/shard_map/row_picks/pallas_call | solution.py:117
  9.4 4.5 %listed_rows.2 = (bf16[1,192,1024]{2,1,0:T(8,128)(2,1)S(1)}, bf16[256,1024]{1,0:T(8,128)(2,1)S(1)}) custom-call(s32[6]{0:T(128)S(1)} %stack.94.where_ref, bf16[448,2048]{1,0:T(8,128)(2,1)S(1)} %row_picks.1.pick_ref, bf16[2048,2048]{1,0:T(8,128)(2,1)} %bitcast.33), custom_call_target="tpu_custom_call" | custom-call | flops 1 | bytes 1 | tf_op jit(solution)/shard_map/listed_rows/pallas_call | solution.py:141
  13.9 1.6 %collective-permute-start.4 = (bf16[1,192,1024]{2,1,0:T(8,128)(2,1)S(1)}, bf16[1,192,1024]{2,1,0:T(8,128)(2,1)S(1)}, u32[]{:S(2)}, u32[]{:S(2)}) collective-permute-start(bf16[1,192,1024]{2,1,0:T(8,128)(2,1)S(1)} %get-tuple-element.30), channel_id=1, source_target_pairs={{0,16},{16,0},{1,17},{17,1},{2,18},{18,2},{3,19},{19,3},{4,20},{20... | collective-permute-start | bytes 1179656 | tf_op jit(solution)/shard_map/ppermute | solution.py:35
  15.6 0.8 collective-permute-done.refs_7_
  16.3 1.5 %collective-permute-start.2 = (bf16[2,2,128,384]{3,2,1,0:T(8,128)(2,1)S(1)}, bf16[2,2,128,384]{3,2,1,0:T(8,128)(2,1)S(1)}, u32[]{:S(2)}, u32[]{:S(2)}) collective-permute-start(bf16[2,2,128,384]{3,2,1,0:T(8,128)(2,1)S(1)} %pad_maximum_fusion.1), channel_id=1, source_target_pairs={{0,2},{1,3},{2,0},{3,1},{4,6},{5,7},{6,4},{7,5},{8,10},{9,11},{10,... | collective-permute-start | bytes 1179656 | tf_op jit(solution)/shard_map/ppermute | solution.py:35
  17.9 4.5 %listed_rows.3 = (bf16[1,192,1024]{2,1,0:T(8,128)(2,1)S(1)}, bf16[256,1024]{1,0:T(8,128)(2,1)S(1)}) custom-call(s32[6]{0:T(128)S(1)} %stack.94.where_ref, bf16[448,2048]{1,0:T(8,128)(2,1)S(1)} %row_picks.1.pick_ref, bf16[2048,2048]{1,0:T(8,128)(2,1)} %bitcast.34), custom_call_target="tpu_custom_call" | custom-call | flops 1 | bytes 1 | tf_op jit(solution)/shard_map/listed_rows/pallas_call | solution.py:141
  22.4 1.6 %collective-permute-start.3 = (bf16[1,192,1024]{2,1,0:T(8,128)(2,1)S(1)}, bf16[1,192,1024]{2,1,0:T(8,128)(2,1)S(1)}, u32[]{:S(2)}, u32[]{:S(2)}) collective-permute-start(bf16[1,192,1024]{2,1,0:T(8,128)(2,1)S(1)} %get-tuple-element.27), channel_id=1, source_target_pairs={{0,16},{16,0},{1,17},{17,1},{2,18},{18,2},{3,19},{19,3},{4,20},{20... | collective-permute-start | bytes 1179656 | tf_op jit(solution)/shard_map/ppermute | solution.py:35
  23.9 0.5 collective-permute-start.10
  24.4 1.0 collective-permute-done.4.refs_0_
  25.4 1.0 merged_rows.3
  26.4 1.1 collective-permute-start.6
  27.5 1.1 collective-permute-start.5
  28.6 4.1 %collective-permute-done.3.refs_0_ = bf16[1,192,1024]{2,1,0:T(8,128)(2,1)S(1)} collective-permute-done((bf16[1,192,1024]{2,1,0:T(8,128)(2,1)S(1)}, bf16[1,192,1024]{2,1,0:T(8,128)(2,1)S(1)}, u32[]{:S(2)}, u32[]{:S(2)}) %collective-permute-start.3) | collective-permute-done | bytes 393248 | tf_op jit(solution)/shard_map/ppermute | solution.py:35
  32.7 1.0 merged_rows.2
  33.8 0.1 collective-permute-start.9
  33.9 0.1 collective-permute-done.10.refs_8_
  34.1 1.5 %collective-permute-start.11 = (bf16[2,2,128,384]{3,2,1,0:T(8,128)(2,1)S(1)}, bf16[2,2,128,384]{3,2,1,0:T(8,128)(2,1)S(1)}, u32[]{:S(2)}, u32[]{:S(2)}) collective-permute-start(bf16[2,2,128,384]{3,2,1,0:T(8,128)(2,1)S(1)} %pad_maximum_fusion.3), channel_id=1, source_target_pairs={{0,2},{1,3},{2,0},{3,1},{4,6},{5,7},{6,4},{7,5},{8,10},{9,11},{10,... | collective-permute-start | bytes 1179656 | tf_op jit(solution)/shard_map/ppermute | solution.py:35
  35.6 0.5 collective-permute-start.7
  36.0 12.7 %collective-permute-done.5.refs_1_ = bf16[2,2,256,128]{3,2,1,0:T(8,128)(2,1)S(1)} collective-permute-done((bf16[2,2,256,128]{3,2,1,0:T(8,128)(2,1)S(1)}, bf16[2,2,256,128]{3,2,1,0:T(8,128)(2,1)S(1)}, u32[]{:S(2)}, u32[]{:S(2)}) %collective-permute-start.5) | collective-permute-done | bytes 262176 | tf_op jit(solution)/shard_map/ppermute | solution.py:35
  48.9 2.3 %forward_values.1 = (f32[256,384]{1,0:T(8,128)S(1)}, f32[256,384]{1,0:T(8,128)S(1)}, f32[256,384]{1,0:T(8,128)S(1)}, f32[256,384]{1,0:T(8,128)S(1)}) custom-call(s32[6]{0:T(128)S(1)} %stack.94.where_ref, bf16[2,2,256,128]{3,2,1,0:T(8,128)(2,1)S(1)} %get-tuple-element.28.refs_0_, bf16[2,2,256,128]{3,2,1,0:T(8,128)(2,1)S(1)} %get-tuple-element.33.refs_1_, ...), custom_call_target="tpu_custom_call" | custom-call | flops 1 | bytes 1 | tf_op jit(solution)/shard_map/forward_values/pallas_call | solution.py:217
  51.2 0.1 collective-permute-start.12
  51.3 0.5 collective-permute-start.13
  51.9 0.1 collective-permute-start.8
  52.7 0.3 collective-permute-done.12.gate_other_ref
  53.0 0.6 collective-permute-done.13.up_other_ref
  53.5 0.8 deltas.1
  54.4 1.5 %collective-permute-start.14 = (bf16[256,384]{1,0:T(8,128)(2,1)S(1)}, bf16[256,384]{1,0:T(8,128)(2,1)S(1)}, u32[]{:S(2)}, u32[]{:S(2)}) collective-permute-start(bf16[256,384]{1,0:T(8,128)(2,1)S(1)} %get-tuple-element.38), channel_id=1, source_target_pairs={{0,2},{1,3},{2,0},{3,1},{4,6},{5,7},{6,4},{7,5},{8,10},{9,11},{10,... | collective-permute-start | bytes 589832 | tf_op jit(solution)/shard_map/ppermute | solution.py:35
  55.9 2.0 %collective-permute-start.20 = (bf16[256,384]{1,0:T(8,128)(2,1)S(1)}, bf16[256,384]{1,0:T(8,128)(2,1)S(1)}, u32[]{:S(2)}, u32[]{:S(2)}) collective-permute-start(bf16[256,384]{1,0:T(8,128)(2,1)S(1)} %get-tuple-element.40), channel_id=1, source_target_pairs={{0,8},{1,9},{2,10},{3,11},{4,12},{5,13},{6,14},{7,15},{8,0},{9,1},... | collective-permute-start | bytes 589832 | tf_op jit(solution)/shard_map/ppermute | solution.py:35
  57.9 3.5 %collective-permute-done.14 = bf16[256,384]{1,0:T(8,128)(2,1)S(1)} collective-permute-done((bf16[256,384]{1,0:T(8,128)(2,1)S(1)}, bf16[256,384]{1,0:T(8,128)(2,1)S(1)}, u32[]{:S(2)}, u32[]{:S(2)}) %collective-permute-start.14) | collective-permute-done | bytes 196640 | tf_op jit(solution)/shard_map/ppermute | solution.py:35
  61.4 4.0 %collective-permute-done.17 = bf16[256,384]{1,0:T(8,128)(2,1)S(1)} collective-permute-done((bf16[256,384]{1,0:T(8,128)(2,1)S(1)}, bf16[256,384]{1,0:T(8,128)(2,1)S(1)}, u32[]{:S(2)}, u32[]{:S(2)}) %collective-permute-start.17) | collective-permute-done | bytes 196640 | tf_op jit(solution)/shard_map/ppermute | solution.py:35
  65.4 0.4 collective-permute-start.21
  65.9 0.6 collective-permute-start.15
  66.5 2.5 %collective-permute-start.18 = (bf16[256,384]{1,0:T(8,128)(2,1)S(1)}, bf16[256,384]{1,0:T(8,128)(2,1)S(1)}, u32[]{:S(2)}, u32[]{:S(2)}) collective-permute-start(bf16[256,384]{1,0:T(8,128)(2,1)S(1)} %collective-permute-done.14), channel_id=1, source_target_pairs={{0,4},{1,5},{2,6},{3,7},{4,0},{5,1},{6,2},{7,3},{8,12},{9,13},{10,... | collective-permute-start | bytes 589832 | tf_op jit(solution)/shard_map/ppermute | solution.py:35
  69.0 1.4 %collective-permute-done.20 = bf16[256,384]{1,0:T(8,128)(2,1)S(1)} collective-permute-done((bf16[256,384]{1,0:T(8,128)(2,1)S(1)}, bf16[256,384]{1,0:T(8,128)(2,1)S(1)}, u32[]{:S(2)}, u32[]{:S(2)}) %collective-permute-start.20) | collective-permute-done | bytes 196640 | tf_op jit(solution)/shard_map/ppermute | solution.py:35
  70.4 5.9 %collective-permute-done.21 = bf16[256,384]{1,0:T(8,128)(2,1)S(1)} collective-permute-done((bf16[256,384]{1,0:T(8,128)(2,1)S(1)}, bf16[256,384]{1,0:T(8,128)(2,1)S(1)}, u32[]{:S(2)}, u32[]{:S(2)}) %collective-permute-start.21) | collective-permute-done | bytes 196640 | tf_op jit(solution)/shard_map/ppermute | solution.py:35
  76.3 0.4 collective-permute-done.18
  76.9 0.5 collective-permute-start.22
  77.4 0.1 collective-permute-start.19
  77.6 9.9 %collective-permute-done.23.refs_13_ = bf16[2,256,384]{2,1,0:T(8,128)(2,1)S(1)} collective-permute-done((bf16[2,256,384]{2,1,0:T(8,128)(2,1)S(1)}, bf16[2,256,384]{2,1,0:T(8,128)(2,1)S(1)}, u32[]{:S(2)}, u32[]{:S(2)}) %collective-permute-start.23) | collective-permute-done | bytes 393248 | tf_op jit(solution)/shard_map/ppermute | solution.py:35
  87.5 1.7 %collective-permute-done.24.refs_14_ = bf16[2,256,384]{2,1,0:T(8,128)(2,1)S(1)} collective-permute-done((bf16[2,256,384]{2,1,0:T(8,128)(2,1)S(1)}, bf16[2,256,384]{2,1,0:T(8,128)(2,1)S(1)}, u32[]{:S(2)}, u32[]{:S(2)}) %collective-permute-start.24) | collective-permute-done | bytes 393248 | tf_op jit(solution)/shard_map/ppermute | solution.py:35
  89.2 0.6 collective-permute-done.15.refs_6_
  89.8 3.3 %gradient_products.1 = f32[16,16]{1,0:T(8,128)S(1)} custom-call(s32[6]{0:T(128)S(1)} %stack.94.where_ref, bf16[2,2,256,128]{3,2,1,0:T(8,128)(2,1)S(1)} %get-tuple-element.28.refs_0_, bf16[2,2,256,128]{3,2,1,0:T(8,128)(2,1)S(1)} %collective-permute-done.5.refs_1_, bf16[2,2,256,128]{3,2,1,0:T(8,128)(2,1)S(1)} %collective-permute-done.6.refs_2_, ...), custom_call_target="tpu_custom_call" | custom-call | flops 1 | bytes 1 | tf_op jit(solution)/shard_map/gradient_products/pallas_call | solution.py:327
  93.2 1.2 collective-permute-done.25
  94.3 2.5 %collective-permute-start.26 = (f32[16,16]{1,0:T(8,128)S(1)}, f32[16,16]{1,0:T(8,128)S(1)}, u32[]{:S(2)}, u32[]{:S(2)}) collective-permute-start(f32[16,16]{1,0:T(8,128)S(1)} %add.31), channel_id=1, source_target_pairs={{0,4},{1,5},{2,6},{3,7},{4,0},{5,1},{6,2},{7,3},{8,12},{9,13},{10,... | collective-permute-start | bytes 3080 | tf_op jit(solution)/shard_map/ppermute | solution.py:35
  96.8 1.6 %collective-permute-done.26 = f32[16,16]{1,0:T(8,128)S(1)} collective-permute-done((f32[16,16]{1,0:T(8,128)S(1)}, f32[16,16]{1,0:T(8,128)S(1)}, u32[]{:S(2)}, u32[]{:S(2)}) %collective-permute-start.26) | collective-permute-done | bytes 1056 | tf_op jit(solution)/shard_map/ppermute | solution.py:35
  98.4 2.0 %collective-permute-start.27 = (f32[16,16]{1,0:T(8,128)S(1)}, f32[16,16]{1,0:T(8,128)S(1)}, u32[]{:S(2)}, u32[]{:S(2)}) collective-permute-start(f32[16,16]{1,0:T(8,128)S(1)} %add.32), channel_id=1, source_target_pairs={{0,8},{1,9},{2,10},{3,11},{4,12},{5,13},{6,14},{7,15},{8,0},{9,1},... | collective-permute-start | bytes 3080 | tf_op jit(solution)/shard_map/ppermute | solution.py:35
  100.5 2.5 %collective-permute-done.27 = f32[16,16]{1,0:T(8,128)S(1)} collective-permute-done((f32[16,16]{1,0:T(8,128)S(1)}, f32[16,16]{1,0:T(8,128)S(1)}, u32[]{:S(2)}, u32[]{:S(2)}) %collective-permute-start.27) | collective-permute-done | bytes 1056 | tf_op jit(solution)/shard_map/ppermute | solution.py:35
  103.0 2.4 %combined_gradient.3 = f32[128,384]{1,0:T(8,128)} custom-call(s32[6]{0:T(128)S(1)} %stack.94.where_ref, f32[16,16]{1,0:T(8,128)S(1)} %add.33.gram_ref, bf16[2,2,256,128]{3,2,1,0:T(8,128)(2,1)S(1)} %get-tuple-element.28.refs_0_, bf16[2,2,256,128]{3,2,1,0:T(8,128)(2,1)S(1)} %collective-permute-done.5.refs_1_, ...), custom_call_target="tpu_custom_call" | custom-call | flops 1 | bytes 1 | tf_op jit(solution)/shard_map/combined_gradient/pallas_call | solution.py:376
  105.4 0.5 collective-permute-start.28
  106.0 0.9 copy-done.1
  106.9 0.9 copy-done.3
  107.9 0.9 copy-done.5
  108.8 1.0 copy-done.7
  109.8 1.0 copy-done.9
  110.8 1.0 copy-done.11
  111.8 1.0 copy-done.13
  112.8 1.0 copy-done.15
  113.8 1.7 %combined_gradient.2 = f32[128,384]{1,0:T(8,128)S(1)} custom-call(s32[6]{0:T(128)S(1)} %stack.94.where_ref, f32[16,16]{1,0:T(8,128)S(1)} %add.33.gram_ref, bf16[2,2,256,128]{3,2,1,0:T(8,128)(2,1)S(1)} %get-tuple-element.28.refs_0_, bf16[2,2,256,128]{3,2,1,0:T(8,128)(2,1)S(1)} %copy-done.3, bf16[2,2,256,128]{3,2,1,0:T(8,128)(2,1)S(1)} %copy-done.1, ...), custom_call_target="tpu_custom_call" | custom-call | flops 1 | bytes 1 | tf_op jit(solution)/shard_map/combined_gradient/pallas_call | solution.py:376
  115.5 2.6 %multiply_subtract_fusion = (f32[1,2,128,384]{3,2,1,0:T(8,128)}, f32[1,2,128,384]{3,2,1,0:T(8,128)}, f32[1,2,128,384]{3,2,1,0:T(8,128)}) fusion(f32[1,2,128,384]{3,2,1,0:T(8,128)} %param.11, f32[1,1,128,384]{3,2,1,0:T(8,128)S(1)} %bitcast.24, f32[1,1,128,384]{3,2,1,0:T(8,128)} %bitcast.19, pred[]{:T(512)S(6)} %eq.3, f32[1,2,128,384]{3,2,1,0:T(8,128)} %param.12, ...), kind=kLoop, calls=%fused_computation.10 | loop fusion | flops 1769472 | bytes 2752513 | tf_op jit(solution)/shard_map/sub | solution.py:59
  (64 shorter events, 0.8 us)
Async XLA Ops:
  0.6 14.9 %copy-start.17 = (f32[1,2,128,384]{3,2,1,0:T(8,128)S(1)}, f32[1,2,128,384]{3,2,1,0:T(8,128)}, u32[]{:S(2)}) copy-start(f32[1,2,128,384]{3,2,1,0:T(8,128)} %param.11) | copy-start | bytes 1179652
  1.7 13.8 %collective-permute-start.1 = (bf16[2,128,384]{2,1,0:T(8,128)(2,1)S(1)}, bf16[2,128,384]{2,1,0:T(8,128)(2,1)S(1)}, u32[]{:S(2)}, u32[]{:S(2)}) collective-permute-start(bf16[2,128,384]{2,1,0:T(8,128)(2,1)S(1)} %convert_bitcast_fusion.refs_5_), channel_id=1, source_target_pairs={{0,4},{1,5},{2,6},{3,7},{4,0},{5,1},{6,2},{7,3},{8,12},{9,13},{10,... | collective-permute-start | bytes 589832 | tf_op jit(solution)/shard_map/ppermute | solution.py:35
  4.8 11.5 %collective-permute-start = (bf16[2,128,384]{2,1,0:T(8,128)(2,1)S(1)}, bf16[2,128,384]{2,1,0:T(8,128)(2,1)S(1)}, u32[]{:S(2)}, u32[]{:S(2)}) collective-permute-start(bf16[2,128,384]{2,1,0:T(8,128)(2,1)S(1)} %convert_bitcast_fusion.refs_5_), channel_id=1, source_target_pairs={{0,8},{1,9},{2,10},{3,11},{4,12},{5,13},{6,14},{7,15},{8,0},{9,1},... | collective-permute-start | bytes 589832 | tf_op jit(solution)/shard_map/ppermute | solution.py:35
  13.9 11.5 %collective-permute-start.4 = (bf16[1,192,1024]{2,1,0:T(8,128)(2,1)S(1)}, bf16[1,192,1024]{2,1,0:T(8,128)(2,1)S(1)}, u32[]{:S(2)}, u32[]{:S(2)}) collective-permute-start(bf16[1,192,1024]{2,1,0:T(8,128)(2,1)S(1)} %get-tuple-element.30), channel_id=1, source_target_pairs={{0,16},{16,0},{1,17},{17,1},{2,18},{18,2},{3,19},{19,3},{4,20},{20... | collective-permute-start | bytes 1179656 | tf_op jit(solution)/shard_map/ppermute | solution.py:35
  16.3 37.2 %copy-start.16 = (bf16[1,1,256,384]{3,2,1,0:T(8,128)(2,1)S(1)}, bf16[1,1,256,384]{3,2,1,0:T(8,128)(2,1)}, u32[]{:S(2)}) copy-start(bf16[1,1,256,384]{3,2,1,0:T(8,128)(2,1)} %param.10) | copy-start | bytes 589828
  16.3 12.3 %collective-permute-start.2 = (bf16[2,2,128,384]{3,2,1,0:T(8,128)(2,1)S(1)}, bf16[2,2,128,384]{3,2,1,0:T(8,128)(2,1)S(1)}, u32[]{:S(2)}, u32[]{:S(2)}) collective-permute-start(bf16[2,2,128,384]{3,2,1,0:T(8,128)(2,1)S(1)} %pad_maximum_fusion.1), channel_id=1, source_target_pairs={{0,2},{1,3},{2,0},{3,1},{4,6},{5,7},{6,4},{7,5},{8,10},{9,11},{10,... | collective-permute-start | bytes 1179656 | tf_op jit(solution)/shard_map/ppermute | solution.py:35
  22.4 10.3 %collective-permute-start.3 = (bf16[1,192,1024]{2,1,0:T(8,128)(2,1)S(1)}, bf16[1,192,1024]{2,1,0:T(8,128)(2,1)S(1)}, u32[]{:S(2)}, u32[]{:S(2)}) collective-permute-start(bf16[1,192,1024]{2,1,0:T(8,128)(2,1)S(1)} %get-tuple-element.27), channel_id=1, source_target_pairs={{0,16},{16,0},{1,17},{17,1},{2,18},{18,2},{3,19},{19,3},{4,20},{20... | collective-permute-start | bytes 1179656 | tf_op jit(solution)/shard_map/ppermute | solution.py:35
  23.9 10.1 %collective-permute-start.10 = (bf16[2,128,384]{2,1,0:T(8,128)(2,1)S(1)}, bf16[2,128,384]{2,1,0:T(8,128)(2,1)S(1)}, u32[]{:S(2)}, u32[]{:S(2)}) collective-permute-start(bf16[2,128,384]{2,1,0:T(8,128)(2,1)S(1)} %collective-permute-done.refs_7_), channel_id=1, source_target_pairs={{0,4},{1,5},{2,6},{3,7},{4,0},{5,1},{6,2},{7,3},{8,12},{9,13},{10,... | collective-permute-start | bytes 589832 | tf_op jit(solution)/shard_map/ppermute | solution.py:35
  26.4 22.4 %collective-permute-start.6 = (bf16[2,2,256,128]{3,2,1,0:T(8,128)(2,1)S(1)}, bf16[2,2,256,128]{3,2,1,0:T(8,128)(2,1)S(1)}, u32[]{:S(2)}, u32[]{:S(2)}) collective-permute-start(bf16[2,2,256,128]{3,2,1,0:T(8,128)(2,1)S(1)} %get-tuple-element.32.refs_3_), channel_id=1, source_target_pairs={{0,12},{1,13},{2,14},{3,15},{4,8},{5,9},{6,10},{7,11},{8,4},{9,5},... | collective-permute-start | bytes 786440 | tf_op jit(solution)/shard_map/ppermute | solution.py:35
  27.5 21.3 %collective-permute-start.5 = (bf16[2,2,256,128]{3,2,1,0:T(8,128)(2,1)S(1)}, bf16[2,2,256,128]{3,2,1,0:T(8,128)(2,1)S(1)}, u32[]{:S(2)}, u32[]{:S(2)}) collective-permute-start(bf16[2,2,256,128]{3,2,1,0:T(8,128)(2,1)S(1)} %get-tuple-element.31.refs_2_), channel_id=1, source_target_pairs={{0,8},{1,9},{2,10},{3,11},{4,12},{5,13},{6,14},{7,15},{8,0},{9,1},... | collective-permute-start | bytes 786440 | tf_op jit(solution)/shard_map/ppermute | solution.py:35
  33.8 15.0 %collective-permute-start.9 = (bf16[4,2,256,128]{3,2,1,0:T(8,128)(2,1)S(1)}, bf16[4,2,256,128]{3,2,1,0:T(8,128)(2,1)S(1)}, u32[]{:S(2)}, u32[]{:S(2)}) collective-permute-start(bf16[4,2,256,128]{3,2,1,0:T(8,128)(2,1)S(1)} %pad_maximum_fusion), channel_id=1, source_target_pairs={{0,1},{1,0},{2,3},{3,2},{4,5},{5,4},{6,7},{7,6},{8,9},{9,8},{10,11... | collective-permute-start | bytes 1572872 | tf_op jit(solution)/shard_map/ppermute | solution.py:35
  34.1 14.8 %collective-permute-start.11 = (bf16[2,2,128,384]{3,2,1,0:T(8,128)(2,1)S(1)}, bf16[2,2,128,384]{3,2,1,0:T(8,128)(2,1)S(1)}, u32[]{:S(2)}, u32[]{:S(2)}) collective-permute-start(bf16[2,2,128,384]{3,2,1,0:T(8,128)(2,1)S(1)} %pad_maximum_fusion.3), channel_id=1, source_target_pairs={{0,2},{1,3},{2,0},{3,1},{4,6},{5,7},{6,4},{7,5},{8,10},{9,11},{10,... | collective-permute-start | bytes 1179656 | tf_op jit(solution)/shard_map/ppermute | solution.py:35
  35.6 16.2 %collective-permute-start.7 = (bf16[2,2,256,128]{3,2,1,0:T(8,128)(2,1)S(1)}, bf16[2,2,256,128]{3,2,1,0:T(8,128)(2,1)S(1)}, u32[]{:S(2)}, u32[]{:S(2)}) collective-permute-start(bf16[2,2,256,128]{3,2,1,0:T(8,128)(2,1)S(1)} %get-tuple-element.33.refs_1_), channel_id=1, source_target_pairs={{0,4},{1,5},{2,6},{3,7},{4,0},{5,1},{6,2},{7,3},{8,12},{9,13},{10,... | collective-permute-start | bytes 786440 | tf_op jit(solution)/shard_map/ppermute | solution.py:35
  48.8 54.2 %copy-start.2 = (bf16[2,2,256,128]{3,2,1,0:T(8,128)(2,1)}, bf16[2,2,256,128]{3,2,1,0:T(8,128)(2,1)S(1)}, u32[]{:S(2)}) copy-start(bf16[2,2,256,128]{3,2,1,0:T(8,128)(2,1)S(1)} %collective-permute-done.5.refs_1_) | copy-start | bytes 786436
  48.8 56.6 %copy-start = (bf16[2,2,256,128]{3,2,1,0:T(8,128)(2,1)}, bf16[2,2,256,128]{3,2,1,0:T(8,128)(2,1)S(1)}, u32[]{:S(2)}) copy-start(bf16[2,2,256,128]{3,2,1,0:T(8,128)(2,1)S(1)} %collective-permute-done.6.refs_2_) | copy-start | bytes 786436
  51.2 1.8 %collective-permute-start.12 = (f32[256,384]{1,0:T(8,128)S(1)}, f32[256,384]{1,0:T(8,128)S(1)}, u32[]{:S(2)}, u32[]{:S(2)}) collective-permute-start(f32[256,384]{1,0:T(8,128)S(1)} %get-tuple-element.36), channel_id=1, source_target_pairs={{0,1},{1,0},{2,3},{3,2},{4,5},{5,4},{6,7},{7,6},{8,9},{9,8},{10,11... | collective-permute-start | bytes 1179656 | tf_op jit(solution)/shard_map/ppermute | solution.py:35
  51.3 2.3 %collective-permute-start.13 = (f32[256,384]{1,0:T(8,128)S(1)}, f32[256,384]{1,0:T(8,128)S(1)}, u32[]{:S(2)}, u32[]{:S(2)}) collective-permute-start(f32[256,384]{1,0:T(8,128)S(1)} %get-tuple-element.37), channel_id=1, source_target_pairs={{0,1},{1,0},{2,3},{3,2},{4,5},{5,4},{6,7},{7,6},{8,9},{9,8},{10,11... | collective-permute-start | bytes 1179656 | tf_op jit(solution)/shard_map/ppermute | solution.py:35
  51.8 53.6 %copy-start.4 = (bf16[2,2,256,128]{3,2,1,0:T(8,128)(2,1)}, bf16[2,2,256,128]{3,2,1,0:T(8,128)(2,1)S(1)}, u32[]{:S(2)}) copy-start(bf16[2,2,256,128]{3,2,1,0:T(8,128)(2,1)S(1)} %collective-permute-done.7.refs_3_) | copy-start | bytes 786436
  51.9 14.0 %collective-permute-start.8 = (bf16[3,2,256,128]{3,2,1,0:T(8,128)(2,1)S(1)}, bf16[3,2,256,128]{3,2,1,0:T(8,128)(2,1)S(1)}, u32[]{:S(2)}, u32[]{:S(2)}) collective-permute-start(bf16[3,2,256,128]{3,2,1,0:T(8,128)(2,1)S(1)} %pad_maximum_fusion.2), channel_id=1, source_target_pairs={{0,1},{1,0},{2,3},{3,2},{4,5},{5,4},{6,7},{7,6},{8,9},{9,8},{10,11... | collective-permute-start | bytes 1179656 | tf_op jit(solution)/shard_map/ppermute | solution.py:35
  54.4 7.0 %collective-permute-start.14 = (bf16[256,384]{1,0:T(8,128)(2,1)S(1)}, bf16[256,384]{1,0:T(8,128)(2,1)S(1)}, u32[]{:S(2)}, u32[]{:S(2)}) collective-permute-start(bf16[256,384]{1,0:T(8,128)(2,1)S(1)} %get-tuple-element.38), channel_id=1, source_target_pairs={{0,2},{1,3},{2,0},{3,1},{4,6},{5,7},{6,4},{7,5},{8,10},{9,11},{10,... | collective-permute-start | bytes 589832 | tf_op jit(solution)/shard_map/ppermute | solution.py:35
  55.8 9.6 %collective-permute-start.17 = (bf16[256,384]{1,0:T(8,128)(2,1)S(1)}, bf16[256,384]{1,0:T(8,128)(2,1)S(1)}, u32[]{:S(2)}, u32[]{:S(2)}) collective-permute-start(bf16[256,384]{1,0:T(8,128)(2,1)S(1)} %get-tuple-element.40), channel_id=1, source_target_pairs={{0,4},{1,5},{2,6},{3,7},{4,0},{5,1},{6,2},{7,3},{8,12},{9,13},{10,... | collective-permute-start | bytes 589832 | tf_op jit(solution)/shard_map/ppermute | solution.py:35
  55.9 14.5 %collective-permute-start.20 = (bf16[256,384]{1,0:T(8,128)(2,1)S(1)}, bf16[256,384]{1,0:T(8,128)(2,1)S(1)}, u32[]{:S(2)}, u32[]{:S(2)}) collective-permute-start(bf16[256,384]{1,0:T(8,128)(2,1)S(1)} %get-tuple-element.40), channel_id=1, source_target_pairs={{0,8},{1,9},{2,10},{3,11},{4,12},{5,13},{6,14},{7,15},{8,0},{9,1},... | collective-permute-start | bytes 589832 | tf_op jit(solution)/shard_map/ppermute | solution.py:35
  65.4 10.9 %collective-permute-start.21 = (bf16[256,384]{1,0:T(8,128)(2,1)S(1)}, bf16[256,384]{1,0:T(8,128)(2,1)S(1)}, u32[]{:S(2)}, u32[]{:S(2)}) collective-permute-start(bf16[256,384]{1,0:T(8,128)(2,1)S(1)} %collective-permute-done.14), channel_id=1, source_target_pairs={{0,8},{1,9},{2,10},{3,11},{4,12},{5,13},{6,14},{7,15},{8,0},{9,1},... | collective-permute-start | bytes 589832 | tf_op jit(solution)/shard_map/ppermute | solution.py:35
  65.9 23.8 %collective-permute-start.15 = (bf16[8,2,256,128]{3,2,1,0:T(8,128)(2,1)S(1)}, bf16[8,2,256,128]{3,2,1,0:T(8,128)(2,1)S(1)}, u32[]{:S(2)}, u32[]{:S(2)}) collective-permute-start(bf16[8,2,256,128]{3,2,1,0:T(8,128)(2,1)S(1)} %constant_dynamic-update-slice_fusion), channel_id=1, source_target_pairs={{0,2},{1,3},{2,0},{3,1},{4,6},{5,7},{6,4},{7,5},{8,10},{9,11},{10,... | collective-permute-start | bytes 3145736 | tf_op jit(solution)/shard_map/ppermute | solution.py:35
  66.5 10.3 %collective-permute-start.18 = (bf16[256,384]{1,0:T(8,128)(2,1)S(1)}, bf16[256,384]{1,0:T(8,128)(2,1)S(1)}, u32[]{:S(2)}, u32[]{:S(2)}) collective-permute-start(bf16[256,384]{1,0:T(8,128)(2,1)S(1)} %collective-permute-done.14), channel_id=1, source_target_pairs={{0,4},{1,5},{2,6},{3,7},{4,0},{5,1},{6,2},{7,3},{8,12},{9,13},{10,... | collective-permute-start | bytes 589832 | tf_op jit(solution)/shard_map/ppermute | solution.py:35
  76.7 10.7 %collective-permute-start.23 = (bf16[2,256,384]{2,1,0:T(8,128)(2,1)S(1)}, bf16[2,256,384]{2,1,0:T(8,128)(2,1)S(1)}, u32[]{:S(2)}, u32[]{:S(2)}) collective-permute-start(bf16[2,256,384]{2,1,0:T(8,128)(2,1)S(1)} %pad_maximum_fusion.6.refs_11_), channel_id=1, source_target_pairs={{0,4},{1,5},{2,6},{3,7},{4,0},{5,1},{6,2},{7,3},{8,12},{9,13},{10,... | collective-permute-start | bytes 1179656 | tf_op jit(solution)/shard_map/ppermute | solution.py:35
  76.8 10.7 %collective-permute-start.16 = (bf16[2,256,384]{2,1,0:T(8,128)(2,1)S(1)}, bf16[2,256,384]{2,1,0:T(8,128)(2,1)S(1)}, u32[]{:S(2)}, u32[]{:S(2)}) collective-permute-start(bf16[2,256,384]{2,1,0:T(8,128)(2,1)S(1)} %pad_maximum_fusion.4.refs_7_), channel_id=1, source_target_pairs={{0,1},{1,0},{2,3},{3,2},{4,5},{5,4},{6,7},{7,6},{8,9},{9,8},{10,11... | collective-permute-start | bytes 1179656 | tf_op jit(solution)/shard_map/ppermute | solution.py:35
  76.9 10.6 %collective-permute-start.22 = (bf16[2,256,384]{2,1,0:T(8,128)(2,1)S(1)}, bf16[2,256,384]{2,1,0:T(8,128)(2,1)S(1)}, u32[]{:S(2)}, u32[]{:S(2)}) collective-permute-start(bf16[2,256,384]{2,1,0:T(8,128)(2,1)S(1)} %pad_maximum_fusion.6.refs_11_), channel_id=1, source_target_pairs={{0,1},{1,0},{2,3},{3,2},{4,5},{5,4},{6,7},{7,6},{8,9},{9,8},{10,11... | collective-permute-start | bytes 1179656 | tf_op jit(solution)/shard_map/ppermute | solution.py:35
  77.4 10.1 %collective-permute-start.19 = (bf16[2,256,384]{2,1,0:T(8,128)(2,1)S(1)}, bf16[2,256,384]{2,1,0:T(8,128)(2,1)S(1)}, u32[]{:S(2)}, u32[]{:S(2)}) collective-permute-start(bf16[2,256,384]{2,1,0:T(8,128)(2,1)S(1)} %pad_maximum_fusion.5.refs_9_), channel_id=1, source_target_pairs={{0,1},{1,0},{2,3},{3,2},{4,5},{5,4},{6,7},{7,6},{8,9},{9,8},{10,11... | collective-permute-start | bytes 1179656 | tf_op jit(solution)/shard_map/ppermute | solution.py:35
  87.5 17.9 %copy-start.6 = (bf16[2,256,384]{2,1,0:T(8,128)(2,1)}, bf16[2,256,384]{2,1,0:T(8,128)(2,1)S(1)}, u32[]{:S(2)}) copy-start(bf16[2,256,384]{2,1,0:T(8,128)(2,1)S(1)} %collective-permute-done.23.refs_13_) | copy-start | bytes 1179652
  87.5 1.7 %collective-permute-start.24 = (bf16[2,256,384]{2,1,0:T(8,128)(2,1)S(1)}, bf16[2,256,384]{2,1,0:T(8,128)(2,1)S(1)}, u32[]{:S(2)}, u32[]{:S(2)}) collective-permute-start(bf16[2,256,384]{2,1,0:T(8,128)(2,1)S(1)} %collective-permute-done.23.refs_13_), channel_id=1, source_target_pairs={{0,1},{1,0},{2,3},{3,2},{4,5},{5,4},{6,7},{7,6},{8,9},{9,8},{10,11... | collective-permute-start | bytes 1179656 | tf_op jit(solution)/shard_map/ppermute | solution.py:35
  87.5 17.9 %copy-start.8 = (bf16[2,256,384]{2,1,0:T(8,128)(2,1)}, bf16[2,256,384]{2,1,0:T(8,128)(2,1)S(1)}, u32[]{:S(2)}) copy-start(bf16[2,256,384]{2,1,0:T(8,128)(2,1)S(1)} %collective-permute-done.16.refs_8_) | copy-start | bytes 1179652
  87.5 17.9 %copy-start.12 = (bf16[2,256,384]{2,1,0:T(8,128)(2,1)}, bf16[2,256,384]{2,1,0:T(8,128)(2,1)S(1)}, u32[]{:S(2)}) copy-start(bf16[2,256,384]{2,1,0:T(8,128)(2,1)S(1)} %collective-permute-done.19.refs_10_) | copy-start | bytes 1179652
  87.5 17.9 %copy-start.10 = (bf16[2,256,384]{2,1,0:T(8,128)(2,1)}, bf16[2,256,384]{2,1,0:T(8,128)(2,1)S(1)}, u32[]{:S(2)}) copy-start(bf16[2,256,384]{2,1,0:T(8,128)(2,1)S(1)} %collective-permute-done.22.refs_12_) | copy-start | bytes 1179652
  89.2 16.2 %copy-start.14 = (bf16[2,256,384]{2,1,0:T(8,128)(2,1)}, bf16[2,256,384]{2,1,0:T(8,128)(2,1)S(1)}, u32[]{:S(2)}) copy-start(bf16[2,256,384]{2,1,0:T(8,128)(2,1)S(1)} %collective-permute-done.24.refs_14_) | copy-start | bytes 1179652
  93.1 1.2 %collective-permute-start.25 = (f32[16,16]{1,0:T(8,128)S(1)}, f32[16,16]{1,0:T(8,128)S(1)}, u32[]{:S(2)}, u32[]{:S(2)}) collective-permute-start(f32[16,16]{1,0:T(8,128)S(1)} %gradient_products.1), channel_id=1, source_target_pairs={{0,1},{1,0},{2,3},{3,2},{4,5},{5,4},{6,7},{7,6},{8,9},{9,8},{10,11... | collective-permute-start | bytes 3080 | tf_op jit(solution)/shard_map/ppermute | solution.py:35
  94.3 4.1 %collective-permute-start.26 = (f32[16,16]{1,0:T(8,128)S(1)}, f32[16,16]{1,0:T(8,128)S(1)}, u32[]{:S(2)}, u32[]{:S(2)}) collective-permute-start(f32[16,16]{1,0:T(8,128)S(1)} %add.31), channel_id=1, source_target_pairs={{0,4},{1,5},{2,6},{3,7},{4,0},{5,1},{6,2},{7,3},{8,12},{9,13},{10,... | collective-permute-start | bytes 3080 | tf_op jit(solution)/shard_map/ppermute | solution.py:35
  98.4 4.5 %collective-permute-start.27 = (f32[16,16]{1,0:T(8,128)S(1)}, f32[16,16]{1,0:T(8,128)S(1)}, u32[]{:S(2)}, u32[]{:S(2)}) collective-permute-start(f32[16,16]{1,0:T(8,128)S(1)} %add.32), channel_id=1, source_target_pairs={{0,8},{1,9},{2,10},{3,11},{4,12},{5,13},{6,14},{7,15},{8,0},{9,1},... | collective-permute-start | bytes 3080 | tf_op jit(solution)/shard_map/ppermute | solution.py:35
  105.4 10.1 %collective-permute-start.28 = (f32[128,384]{1,0:T(8,128)}, f32[128,384]{1,0:T(8,128)}, u32[]{:S(2)}, u32[]{:S(2)}) collective-permute-start(f32[128,384]{1,0:T(8,128)} %combined_gradient.3), channel_id=1, source_target_pairs={{0,2},{1,3},{2,0},{3,1},{4,6},{5,7},{6,4},{7,5},{8,10},{9,11},{10,... | collective-permute-start | bytes 589832 | tf_op jit(solution)/shard_map/ppermute | solution.py:35
  106.0 0.9 copy-start.1
  106.9 0.9 copy-start.3
  107.9 0.9 copy-start.5
  108.8 1.0 copy-start.7
  109.8 1.0 copy-start.9
  110.8 1.0 copy-start.11
  111.8 1.0 copy-start.13
  112.8 1.0 copy-start.15
